TPU v7x, 256 devices: a whole 4x4x8 slice. The times are simulated.
256 devices in a mesh: dp: 4 (over x), ctx: 16 (over y_lo, z), tensor: 4 (over y_hi, core).
Axes of the slice: x: 4, y: 4 (y_hi: 2, y_lo: 2; y = y_hi * 2 + y_lo), z: 8, core: 2. Of those that a mesh axis runs over, the one named last changes fastest.
Arguments:
- layer_in: bfloat16 [4, 4096, 2048], P('dp', 'ctx'), may hold values from -6 to 6
- head_in: bfloat16 [4, 4096, 4096], P('dp', 'ctx', 'tensor'), may hold values from -6 to 6
- step_raw: float32 [4, 4096, 64], P('dp', 'ctx', 'tensor'), may hold values from -4 to 4
- step_bias: float32 [64], P('tensor'), may hold values from -4 to 0
- rate_log: float32 [64], P('tensor'), may hold values from -6 to 0
- skip_gain: float32 [64], P('tensor'), may hold values from 0.2 to 2
- inject_weight: bfloat16 [2048, 8, 256], P('dp', 'tensor'), may hold values from -0.03125 to 0.03125
- out_weight: bfloat16 [2048, 4096], P('dp', 'tensor'), may hold values from -0.125 to 0.125
- upstream: bfloat16 [4, 4096, 2048], P('dp', 'ctx'), may hold values from -6 to 6
- window_start: int32 [4], P('dp'), may hold values from 0 to 1023
- lengths: int32 [4], P('dp'), may hold values from 2048 to 4096
Outputs:
- layer_grad: bfloat16 [4, 4096, 2048], P('dp', 'ctx')
- head_grad: bfloat16 [4, 4096, 4096], P('dp', 'ctx', 'tensor')
- step_grad: float32 [4, 4096, 64], P('dp', 'ctx', 'tensor')
- out_weight_grad: float32 [2048, 4096], P(('dp', 'ctx'), 'tensor')
- inject_weight_grad: float32 [2048, 8, 256], P(('dp', 'ctx'), 'tensor')
All inputs are finite; a program needn't handle non-finite values.
Results may differ from a plain program's by a relative error of at most 0.015.
Values may be sent and summed in bfloat16 or wider, within the bound.
A program may use at most 128 MiB of HBM per device.

v0:
```python
import jax
import jax.numpy as jnp
from jax import lax
from jax.sharding import PartitionSpec as P

BLOCK = 128


highest = lax.Precision.HIGHEST


def entering_2(x, axis, combine, identity, reverse):
    peers, position = (lax.axis_size(axis), lax.axis_index(axis))
    everything = jax.tree.map(lambda part: lax.all_gather(part, axis), x)
    start = jax.tree.map(
        lambda part, zero: jnp.broadcast_to(jnp.asarray(zero, part.dtype), part.shape), x, identity
    )

    def hop(k, before):
        at = peers - 1 - k if reverse else k
        reached = at > position if reverse else at < position
        new = combine(before, jax.tree.map(lambda part: part[at], everything))
        return jax.tree.map(lambda a, b: jnp.where(reached, a, b), new, before)

    return lax.fori_loop(0, peers, hop, start)


def block_parts(head_values, inject, readout, steps, rates):
    log_decay = -steps * rates
    running = jnp.cumsum(log_decay, axis=1)
    scores = jnp.einsum("ctgn,csgn->ctsg", readout, inject, precision=highest)
    spread = running[:, :, None] - running[:, None, :]
    length = running.shape[1]
    causal = (jnp.arange(length)[:, None] >= jnp.arange(length)[None, :])[None, :, :, None, None]
    decays = jnp.exp(jnp.where(causal, spread, -jnp.inf))
    weighted = scores[..., None] * decays * steps[:, None]
    within = jnp.einsum("ctsgj,csgjp->ctgjp", weighted, head_values, precision=highest)
    tail_weight = jnp.exp(running[:, -1:] - running) * steps
    states = jnp.einsum(
        "csgj,csgjp,csgn->cgjpn", tail_weight, head_values, inject, precision=highest
    )
    return (within, states, running[:, -1], running)


def block_outputs(within, states, totals, running, readout, head_values, skip_gain, state_in):

    def advance(carried, pair):
        return (jnp.exp(pair[1])[..., None, None] * carried + pair[0], carried)

    state_out, entering = lax.scan(advance, state_in, (states, totals))
    across = (
        jnp.einsum("ctgn,cgjpn->ctgjp", readout, entering, precision=highest)
        * jnp.exp(running)[..., None]
    )
    return (within + across + skip_gain[None, None, :, :, None] * head_values, state_out)


def layer_piece(values, coded, raw, state_in, masks, step_bias, rates, skip_gain, block_len):
    tokens = values.shape[0]
    groups = coded.shape[1]
    state_width = coded.shape[2] // 2
    heads = raw.shape[1]
    per_group = heads // groups
    head_width = values.shape[1] // heads
    block_count = tokens // block_len
    steps = masks[:, None] * jax.nn.softplus(raw + step_bias)
    head_values = values.reshape(block_count, block_len, groups, per_group, head_width)
    inject = coded[:, :, :state_width].reshape(block_count, block_len, groups, state_width)
    readout = coded[:, :, state_width:].reshape(block_count, block_len, groups, state_width)
    steps_four = steps.reshape(block_count, block_len, groups, per_group)
    within, states, totals, running = block_parts(
        head_values, inject, readout, steps_four, rates.reshape(groups, per_group)
    )
    result, state_out = block_outputs(
        within,
        states,
        totals,
        running,
        readout,
        head_values,
        skip_gain.reshape(groups, per_group),
        state_in,
    )
    result = result * masks.reshape(block_count, block_len)[:, :, None, None, None]
    return (result.reshape(tokens, heads * head_width), state_out)


def chain_step(earlier, later):
    return (earlier[0] + later[0], jnp.exp(later[0])[..., None, None] * earlier[1] + later[1])


def per_device(
    layer_in,
    head_in,
    step_raw,
    step_bias,
    rate_log,
    skip_gain,
    inject_weight,
    out_weight,
    upstream,
    window_start,
    lengths,
):
    tokens = head_in.shape[1]
    heads = rate_log.shape[0]
    groups = inject_weight.shape[1]
    coded_width = inject_weight.shape[2]
    state_width = coded_width // 2
    per_group = heads // groups
    head_width = head_in.shape[2] // heads
    inject_cols = groups * coded_width
    inputs = layer_in[0]
    incoming = upstream[0]
    contract_rows = (((0,), (0,)), ((), ()))
    contract_cols = (((1,), (1,)), ((), ()))
    positions = lax.axis_index("ctx") * tokens + jnp.arange(tokens, dtype=jnp.int32)
    masks = ((positions >= window_start[0]) & (positions < lengths[0])).astype(jnp.float32)
    rates = jnp.exp(rate_log)
    gathered = lax.all_gather(inject_weight, "dp", axis=0, tiled=True).reshape(-1, inject_cols)
    projected = jnp.dot(inputs, gathered, preferred_element_type=jnp.float32).astype(jnp.bfloat16)
    columns = incoming
    back_grad = jnp.dot(
        columns,
        lax.all_gather(out_weight, "dp", axis=0, tiled=True),
        preferred_element_type=jnp.float32,
    ).astype(jnp.bfloat16)
    values = head_in[0].astype(jnp.float32)
    coded = projected.reshape(tokens, groups, coded_width).astype(jnp.float32)
    raw = step_raw[0]
    steps = (masks[:, None] * jax.nn.softplus(raw + step_bias)).reshape(tokens, groups, per_group)
    log_decay = -steps * rates.reshape(groups, per_group)
    running = jnp.cumsum(log_decay, axis=0)
    device_decay = running[-1]
    head_values = values.reshape(tokens, groups, per_group, head_width)
    tail_weight = jnp.exp(device_decay - running) * steps
    own_state = jnp.einsum(
        "tgj,tgjp,tgn->gjpn", tail_weight, head_values, coded[:, :, :state_width], precision=highest
    )
    identity = (jnp.zeros_like(device_decay), jnp.zeros_like(own_state))
    decay_in, state_in = entering_2((device_decay, own_state), "ctx", chain_step, identity, False)
    back_float = back_grad.astype(jnp.float32)
    masked_back = (back_float * masks[:, None]).reshape(tokens, groups, per_group, head_width)
    own_pull = jnp.einsum(
        "tgj,tgjp,tgn->gjpn",
        jnp.exp(running),
        masked_back,
        coded[:, :, state_width:],
        precision=highest,
    )
    decay_out, state_later = entering_2((device_decay, own_pull), "ctx", chain_step, identity, True)

    def forward(values_f, coded_f, raw_f):
        return layer_piece(
            values_f, coded_f, raw_f, state_in, masks, step_bias, rates, skip_gain, BLOCK
        )

    (result, state_out), pullback = jax.vjp(forward, values, coded, raw)
    head_grad, coded_grad, raw_grad = pullback((back_float, state_later))
    rounded = coded_grad.reshape(tokens, inject_cols).astype(jnp.bfloat16)
    result_round = result.astype(jnp.bfloat16)
    partial_value = lax.dot_general(
        rounded, gathered, contract_cols, preferred_element_type=jnp.float32
    )
    layer_grad = lax.psum(partial_value, "tensor").astype(jnp.bfloat16)
    columns = incoming
    weight_grad = lax.psum_scatter(
        lax.dot_general(columns, result_round, contract_rows, preferred_element_type=jnp.float32),
        ("dp", "ctx"),
        scatter_dimension=0,
        tiled=True,
    )
    columns = inputs
    product = lax.dot_general(columns, rounded, contract_rows, preferred_element_type=jnp.float32)
    inject_grad = lax.psum_scatter(
        product.reshape(
            inject_weight.shape[0] // lax.axis_size("ctx") * lax.axis_size(("dp", "ctx")),
            groups,
            coded_width,
        ),
        ("dp", "ctx"),
        scatter_dimension=0,
        tiled=True,
    )
    return (
        layer_grad[None],
        head_grad.astype(jnp.bfloat16)[None],
        raw_grad[None],
        weight_grad,
        inject_grad,
    )


def solution(mesh):
    placed = (
        P("dp", "ctx", None),
        P("dp", "ctx", "tensor"),
        P("dp", "ctx", "tensor"),
        P("tensor"),
        P("tensor"),
        P("tensor"),
        P("dp", "tensor", None),
        P("dp", "tensor"),
        P("dp", "ctx", None),
        P("dp"),
        P("dp"),
    )
    return jax.shard_map(
        per_device,
        mesh=mesh,
        in_specs=placed,
        out_specs=(
            P("dp", "ctx", None),
            P("dp", "ctx", "tensor"),
            P("dp", "ctx", "tensor"),
            P(("dp", "ctx"), "tensor"),
            P(("dp", "ctx"), "tensor", None),
        ),
        check_vma=False,
    )
```

profile of v0, /device:TPU:16, one launch (start us, length us, event | category | flops | bytes accessed | tf_op | source)
XLA Modules:
  0.0 1309.2 jit_solution(2069933607069803915)
XLA Ops:
  7.3 2.0 copy.199
  13.7 33.0 %all-gather.9.cloned.1.call-done = bf16[2048,2,256]{2,0,1:T(8,128)(2,1)} async-done(((bf16[512,2,256]{2,0,1:T(8,128)(2,1)}), bf16[2048,2,256]{2,0,1:T(8,128)(2,1)}) %all-gather.9.cloned.1.call-update) | async-done | bytes 2097168 | tf_op jit(solution)/shard_map/all_gather | solution.py:120
  46.6 4.0 copy.200
  50.6 2.3 convolution_convert_fusion.1
  54.7 44.6 %all-gather.7.cloned.1.call-done = bf16[2048,1024]{1,0:T(8,128)(2,1)} async-done(((bf16[512,1024]{1,0:T(8,128)(2,1)}), bf16[2048,1024]{1,0:T(8,128)(2,1)}) %all-gather.7.cloned.1.call-update) | async-done | bytes 4194320 | tf_op jit(solution)/shard_map/all_gather | solution.py:125
  99.3 4.8 broadcast_multiply_fusion
  107.9 35.7 %all_gather.23 = f32[16,2,8]{2,1,0:T(2,128)} all-gather(f32[1,2,8]{2,1,0:T(2,128)S(1)} %copy.197), channel_id=1, replica_groups=mesh['dp'=4,'ctx'=16,'tensor'=4] {'ctx'}, dimensions={0}, use_global_device_ids=true | all-gather | bytes 1088 | tf_op jit(solution)/shard_map/all_gather | solution.py:14
  148.2 2.8 reshape.301
  151.0 2.4 copy.189
  155.1 4.1 fusion.42
  159.3 43.7 %all-gather.11.cloned.1.call-done = f32[32,8,64,128]{3,2,1,0:T(8,128)} async-done(((f32[2,8,64,128]{3,2,1,0:T(8,128)}), f32[32,8,64,128]{3,2,1,0:T(8,128)}) %all-gather.11.cloned.1.call-update) | async-done | bytes 8388624 | tf_op jit(solution)/shard_map/all_gather | solution.py:14
  203.0 29.9 %while.66 = (s32[]{:T(128)}, f32[2,8,64,128]{3,2,1,0:T(8,128)S(1)}, s32[]{:T(128)}, f32[16,2,8]{2,1,0:T(2,128)}, f32[16,2,8,64,128]{4,3,2,1,0:T(8,128)}, /*index=5*/s32[]{:T(128)}, s32[]{:T(128)}) while((s32[]{:T(128)}, f32[2,8,64,128]{3,2,1,0:T(8,128)S(1)}, s32[]{:T(128)}, f32[16,2,8]{2,1,0:T(2,128)}, ...), condition=%wide.region_4.5_spmd.clone, body=%wide.region_3.4_spmd.clone.sunk | while | flops 524292 | bytes 1573169 | solution.py:25
  233.0 2.6 while.64
  235.7 3.1 convolution_bitcast_fusion.6
  239.8 63.5 %all-gather.13.cloned.1.call-done = f32[32,8,64,128]{3,2,1,0:T(8,128)} async-done(((f32[2,8,64,128]{3,2,1,0:T(8,128)}), f32[32,8,64,128]{3,2,1,0:T(8,128)}) %all-gather.13.cloned.1.call-update) | async-done | bytes 8388624 | tf_op jit(solution)/shard_map/all_gather | solution.py:14
  303.3 29.9 %while.67 = (s32[]{:T(128)}, f32[2,8,64,128]{3,2,1,0:T(8,128)S(1)}, s32[]{:T(128)}, f32[16,2,8]{2,1,0:T(2,128)}, f32[16,2,8,64,128]{4,3,2,1,0:T(8,128)}, /*index=5*/s32[]{:T(128)}, s32[]{:T(128)}, s32[]{:T(128)}, s32[]{:T(128)}) while((s32[]{:T(128)}, f32[2,8,64,128]{3,2,1,0:T(8,128)S(1)}, s32[]{:T(128)}, f32[16,2,8]{2,1,0:T(2,128)}, ...), condition=%wide.region_9.10_spmd.clone, body=%wide.region_8.9_spmd.clone.sunk | while | flops 524296 | bytes 1573231 | solution.py:25
  334.3 4.3 while.65
  338.7 3.1 fusion.43
  343.3 3.9 fusion.50
  347.2 7.2 copy.231
  355.2 2.0 multiply_reduce_fusion.2
  357.1 3.9 fusion.32
  361.6 4.5 convolution_bitcast_fusion
  366.1 9.3 copy.259
  377.4 3.8 convolution_bitcast_fusion.1
  383.5 2.2 fusion.121
  386.6 4.5 fusion.35
  391.1 2.9 copy.256
  394.0 2.6 reshape.302
  397.3 49.7 %all-reduce.9 = bf16[256,2048]{1,0:T(8,128)(2,1)} all-reduce(f32[256,2048]{1,0:T(8,128)S(1)} %copy-done.7), channel_id=1, replica_groups=mesh['dp'=4,'ctx'=16,'tensor'=4] {'tensor'}, use_global_device_ids=true, to_apply=%region_13.14 | all-reduce | flops 524288 | bytes 3145728 | tf_op jit(solution)/shard_map/psum | solution.py:165
  447.0 523.1 %all-reduce.8.cloned.1.call-done = f32[2048,2,256]{2,1,0:T(2,128)} async-done(((f32[2048,2,256]{2,1,0:T(2,128)}), f32[2048,2,256]{2,1,0:T(2,128)}) %all-reduce.8.cloned.1.call-update) | async-done | bytes 4194320
  971.6 330.8 %reduce-scatter.4.cloned.1.call-done = f32[32,1024]{1,0:T(8,128)} async-done(((f32[2048,1024]{1,0:T(8,128)}), f32[32,1024]{1,0:T(8,128)}) %reduce-scatter.4.cloned.1.call-update) | async-done | bytes 131088
  (239 shorter events, 92.1 us)
Async XLA Ops:
  7.2 92.2 %copy-start = (bf16[1,256,2048]{2,1,0:T(8,128)(2,1)S(1)}, bf16[1,256,2048]{2,1,0:T(8,128)(2,1)}, u32[]{:S(2)}) copy-start(bf16[1,256,2048]{2,1,0:T(8,128)(2,1)} %param.27) | copy-start | bytes 3145732
  7.2 4.2 copy-start.36
  7.2 4.3 copy-start.34
  7.2 4.4 copy-start.13
  7.2 5.9 copy-start.12
  7.2 39.4 %all-gather.9.cloned.1.call-start = ((), (), s32[]{:S(2)}) async-start(), calls=%async_computation.2 | async-start | bytes 2621440 | tf_op jit(solution)/shard_map/all_gather | solution.py:120
  9.3 90.0 %all-gather.7.cloned.1.call-start = ((), (), s32[]{:S(2)}) async-start(), calls=%async_computation.1 | async-start | bytes 5242880 | tf_op jit(solution)/shard_map/all_gather | solution.py:125
  10.1 192.9 %all-gather.11.cloned.1.call-start = ((), (), s32[]{:S(2)}) async-start(), calls=%async_computation.3 | async-start | bytes 8912896 | tf_op jit(solution)/shard_map/all_gather | solution.py:14
  11.5 95.9 %copy-start.32 = (f32[2,8]{1,0:T(2,128)}, f32[2,8]{1,0:T(2,128)S(1)}, u32[]{:S(2)}) copy-start(f32[2,8]{1,0:T(2,128)S(1)} %mul.290) | copy-start | bytes 196
  11.6 87.7 %copy-start.26 = (f32[256]{0:T(256)}, f32[256]{0:T(256)S(1)}, u32[]{:S(2)}) copy-start(f32[256]{0:T(256)S(1)} %and_convert_fusion) | copy-start | bytes 3076
  13.6 37.0 %copy-start.11 = (bf16[1,256,2048]{2,1,0:T(8,128)(2,1)S(1)}, bf16[1,256,2048]{2,1,0:T(8,128)(2,1)}, u32[]{:S(2)}) copy-start(bf16[1,256,2048]{2,1,0:T(8,128)(2,1)} %param.19) | copy-start | bytes 3145732
  54.7 248.6 %all-gather.13.cloned.1.call-start = ((), (), s32[]{:S(2)}) async-start(), calls=%async_computation.4 | async-start | bytes 8912896 | tf_op jit(solution)/shard_map/all_gather | solution.py:14
  107.1 863.0 %all-reduce.8.cloned.1.call-start = ((), (), s32[]{:S(2)}) async-start(), calls=%async_computation.6 | async-start | bytes 8388608
  107.3 40.8 %copy-start.4 = (bf16[2,128,2,8,64]{1,0,4,3,2:T(2,128)(2,1)}, bf16[2,128,2,8,64]{1,0,4,3,2:T(2,128)(2,1)S(1)}, u32[]{:S(2)}) copy-start(bf16[2,128,2,8,64]{1,0,4,3,2:T(2,128)(2,1)S(1)} %reshape.277) | copy-start | bytes 1572868
  107.4 36.2 %copy-start.24 = (f32[2,128]{1,0:T(2,128)}, f32[2,128]{1,0:T(2,128)S(1)}, u32[]{:S(2)}) copy-start(f32[2,128]{1,0:T(2,128)S(1)} %and_convert_fusion.1) | copy-start | bytes 3076
  107.5 36.7 %copy-start.22 = (f32[2,128,2,8]{1,3,2,0:T(8,128)}, f32[2,128,2,8]{1,3,2,0:T(8,128)S(1)}, u32[]{:S(2)}) copy-start(f32[2,128,2,8]{1,3,2,0:T(8,128)S(1)} %get-tuple-element.576) | copy-start | bytes 49156
  151.0 4.1 copy-start.28
  153.4 5.9 copy-start.1
  203.0 30.0 %copy-start.18 = (f32[2,2,8]{2,1,0:T(2,128)S(1)}, f32[2,2,8]{2,1,0:T(2,128)}, u32[]{:S(2)}) copy-start(f32[2,2,8]{2,1,0:T(2,128)} %copy-done.17) | copy-start | bytes 388
  203.0 30.0 %copy-start.31 = (f32[2,2,8,1,1]{2,1,4,3,0:T(2,128)S(1)}, f32[2,2,8,1,1]{2,1,4,3,0:T(2,128)}, u32[]{:S(2)}) copy-start(f32[2,2,8,1,1]{2,1,4,3,0:T(2,128)} %custom-call.2) | copy-start | bytes 388
  334.3 4.3 copy-start.6
  334.3 4.3 copy-start.20
  338.6 4.5 copy-start.10
  354.5 947.9 %reduce-scatter.4.cloned.1.call-start = ((), (), s32[]{:S(2)}) async-start(), calls=%async_computation.5 | async-start | bytes 8519680
  355.2 5.8 copy-start.39
  381.2 4.5 copy-start.33
  381.2 5.3 copy-start.2
  381.9 4.7 copy-start.16
  391.1 5.5 copy-start.14
  391.1 5.5 copy-start.27
  391.1 5.5 copy-start.35
  391.1 6.2 copy-start.7
  (14 other events, 29.0 us)
Sparse Core Ops, SparseCore 0:
  10.4 36.1 all-gather.8
  48.4 50.8 all-gather.6
  101.7 101.2 all-gather.10
  204.6 98.6 all-gather.12
  354.6 615.4 all-reduce.7
  973.2 329.0 reduce-scatter.3
where the time goes:
time: 1310 us
  waiting for transfers between devices  1040 us (79%)
  blocking collectives  85.4 us (7%)
  local copies, waits for them, and re-layouts  67.4 us (5%)
  other arithmetic  50.5 us (4%)
  matrix products  48.5 us (4%)
  between operations  16.7 us (1%)
    unnamed x8, waiting for transfers between devices  855 us
    all_gather x2, waiting for transfers between devices, entering_2(): everything = jax.tree.map(lambda part: lax.all_gather(part, axis), x)  107 us
    psum x1, blocking collectives, per_device(): layer_grad = lax.psum(partial_value, 'tensor').astype(jnp.bfloat16)  49.7 us
    all_gather x1, waiting for transfers between devices, per_device(): lax.all_gather(out_weight, 'dp', axis=0, tiled=True)  44.6 us
    select_n x32, other arithmetic, hop(): return jax.tree.map(lambda a, b: jnp.where(reached, a, b), new, before)  37.6 us
    all_gather x1, blocking collectives, entering_2(): everything = jax.tree.map(lambda part: lax.all_gather(part, axis), x)  35.7 us
    all_gather x1, waiting for transfers between devices, per_device(): lax.all_gather(inject_weight, 'dp', axis=0, tiled=True)  33 us
  transfers between devices with their start and end apart: 6, of which 6 were waited for; matrix products, arithmetic and copies ran while one was open for 9% of the time, Pallas kernels for 0%

commit v1 on v0

v1 whole, which is shorter than its diff:
```python
import jax
import jax.numpy as jnp
from jax import lax
from jax.experimental import pallas as pl
from jax.experimental.pallas import tpu as pltpu
from jax.sharding import PartitionSpec as P

f32 = jnp.float32
bf16 = jnp.bfloat16
MESH = pl.DeviceIdType.MESH
ANY = pl.BlockSpec(memory_space=pl.ANY)
VM = pl.BlockSpec(memory_space=pltpu.VMEM)
LIMIT = 56 * 1024 * 1024
ROWS = (((0,), (0,)), ((), ()))
COLS = (((1,), (1,)), ((), ()))


def remote(src, dst, send, recv, where):
    return pltpu.make_async_remote_copy(
        src_ref=src, dst_ref=dst, send_sem=send, recv_sem=recv, device_id=where, device_id_type=MESH
    )


def greet(partners):
    barrier = pltpu.get_barrier_semaphore()
    for where in partners:
        pl.semaphore_signal(barrier, inc=1, device_id=where, device_id_type=MESH)
    pl.semaphore_wait(barrier, len(partners))


def places():
    x = lax.axis_index("dp")
    c = lax.axis_index("ctx")
    t = lax.axis_index("tensor")
    z = lax.rem(c, 8)
    base = c - z
    spots = dict(
        right={"dp": lax.rem(x + 1, 4)},
        left={"dp": lax.rem(x + 3, 4)},
        up={"ctx": base + lax.rem(z + 1, 8)},
        down={"ctx": base + lax.rem(z + 7, 8)},
        across={"ctx": lax.rem(c + 8, 16)},
        core={"tensor": t + 1 - 2 * lax.rem(t, 2)},
        far={"tensor": lax.rem(t + 2, 4)},
    )
    return x, c, t, z, spots


def dot(a, b, dims=None):
    if dims is None:
        return jnp.dot(a, b, preferred_element_type=f32)
    return lax.dot_general(a, b, dims, preferred_element_type=f32)


def pieces(v, count):
    found = []
    for _ in range(count):
        part = v.astype(bf16)
        found.append(part)
        v = v - part.astype(f32)
    return found


def split_left(v, m, count, dims=None):
    return sum(dot(part, m, dims) for part in pieces(v, count))


def split_right(m, v, count, dims=None):
    return sum(dot(m, part, dims) for part in pieces(v, count))


def weights_kernel(
    wi, wo, lin, up, proj, back, winj_out, wi_v, wo_v, lin_v, up_v, send, recv, local
):
    x, c, t, z, at = places()
    h = lax.rem(z, 2)
    lefts, rights, opposite = lax.rem(x + 3, 4), lax.rem(x + 1, 4), lax.rem(x + 2, 4)
    own = [(wi, wi_v), (wo, wo_v)]

    def rows(slab, half, q):
        return pl.ds(pl.multiple_of(slab * 512 + half * 256 + q * 128, 128), 128)

    loads = [
        pltpu.make_async_copy(wi, wi_v.at[pl.ds(pl.multiple_of(x * 512, 512), 512)], local.at[0]),
        pltpu.make_async_copy(wo, wo_v.at[pl.ds(pl.multiple_of(x * 512, 512), 512)], local.at[1]),
        pltpu.make_async_copy(lin, lin_v, local.at[2]),
        pltpu.make_async_copy(up, up_v, local.at[3]),
    ]
    for load in loads:
        load.start()
    greet([at["right"], at["left"], at["up"], at["down"]])

    sent = []

    def first(k, q, event, where):
        src, dst = own[k]
        s = remote(
            src.at[pl.ds(pl.multiple_of(h * 256 + q * 128, 128), 128)],
            dst.at[rows(x, h, q)],
            send.at[k, event],
            recv.at[k, event],
            where,
        )
        s.start()
        sent.append(s)

    def arrived(k, slab, half, q, event):
        dst = own[k][1].at[rows(slab, half, q)]
        remote(dst, dst, send.at[k, event], recv.at[k, event], at["left"]).wait_recv()

    def forward(k, slab, q, event, where):
        dst = own[k][1].at[rows(slab, h, q)]
        s = remote(dst, dst, send.at[k, event], recv.at[k, event], where)
        s.start()
        sent.append(s)

    for k in range(2):
        first(k, 0, 0, at["right"])
        first(k, 1, 2, at["left"])
        first(k, 1, 1, at["right"])
        first(k, 0, 3, at["left"])
    for k in range(2):
        arrived(k, lefts, h, 0, 0)
        forward(k, lefts, 0, 4, at["right"])
        forward(k, lefts, 0, 6, at["up"])
        arrived(k, rights, h, 1, 2)
        forward(k, rights, 1, 5, at["left"])
        forward(k, rights, 1, 10, at["down"])
        arrived(k, lefts, h, 1, 1)
        forward(k, lefts, 1, 9, at["down"])
        arrived(k, rights, h, 0, 3)
        forward(k, rights, 0, 7, at["up"])
    for k in range(2):
        arrived(k, opposite, h, 0, 4)
        forward(k, opposite, 0, 8, at["up"])
        arrived(k, opposite, h, 1, 5)
        forward(k, opposite, 1, 11, at["down"])
    for load in loads:
        load.wait()
    results = [(lin_v, proj), (up_v, back)]
    for k in range(2):
        for n, slab in enumerate((lefts, rights, opposite)):
            arrived(k, slab, 1 - h, 0, 6 + n)
            arrived(k, slab, 1 - h, 1, 9 + n)
        a, out = results[k]
        out[...] = dot(a[...], own[k][1][...]).astype(bf16)
        if k == 0:
            keep = pltpu.make_async_copy(wi_v, winj_out, local.at[0])
            keep.start()
    keep.wait()
    for s in sent:
        s.wait_send()


def weights_call(wi, wo, lin, up):
    return pl.pallas_call(
        weights_kernel,
        out_shape=(
            jax.ShapeDtypeStruct((256, 512), bf16),
            jax.ShapeDtypeStruct((256, 1024), bf16),
            jax.ShapeDtypeStruct((2048, 512), bf16),
        ),
        in_specs=[ANY] * 4,
        out_specs=(VM, VM, ANY),
        scratch_shapes=[
            pltpu.VMEM((2048, 512), bf16),
            pltpu.VMEM((2048, 1024), bf16),
            pltpu.VMEM((256, 2048), bf16),
            pltpu.VMEM((256, 2048), bf16),
            pltpu.SemaphoreType.DMA((2, 12)),
            pltpu.SemaphoreType.DMA((2, 12)),
            pltpu.SemaphoreType.DMA((4,)),
        ],
        compiler_params=pltpu.CompilerParams(
            collective_id=1, has_side_effects=True, vmem_limit_bytes=LIMIT
        ),
        name="weights",
    )(wi, wo, lin, up)


def iota(shape, axis):
    return lax.broadcasted_iota(jnp.int32, shape, axis)


def scan_kernel(
    x_ref, dt_ref, sig_ref, mask_ref, par_ref, proj_ref, back_ref, lin, up,
    res_ref, rnd_ref, hg_ref, sg_ref, linq, upq,
    y_s, z_s, xs_s, dy_s, ds_s, r_s, rt_s, msg, got, out, fin,
    send1, recv1, send2, recv2, send3, recv3, local,
):
    x, c, t, z, at = places()
    peers = [{"ctx": lax.rem(c + k, 16)} for k in range(1, 16)]
    greet(peers + [{"dp": lax.rem(x + k, 4)} for k in range(1, 4)])

    def quarter(j):
        return pl.ds(pl.multiple_of(j * 512, 512), 512)

    acts = []
    for n, (src, dst) in enumerate(((up, upq), (lin, linq))):
        for k in (1, 3, 2):
            to = lax.rem(x + k, 4)
            acts.append(
                remote(
                    src.at[:, quarter(to)], dst.at[x], send3.at[n, k], recv3.at[n, k], {"dp": to}
                )
            )
    own_up = pltpu.make_async_copy(up.at[:, quarter(x)], upq.at[x], local.at[0])
    own_lin = pltpu.make_async_copy(lin.at[:, quarter(x)], linq.at[x], local.at[1])
    own_up.start()
    own_lin.start()

    expand = jnp.where(
        (iota((128, 1024), 1) >= iota((128, 1024), 0) * 64)
        & (iota((128, 1024), 1) < iota((128, 1024), 0) * 64 + 64),
        1.0,
        0.0,
    ).astype(bf16)
    above = iota((256, 256), 0) >= iota((256, 256), 1)
    tril = jnp.where(above, 1.0, 0.0).astype(bf16)
    rate = par_ref[0:1, :]
    dt = dt_ref[...]
    running = split_right(tril, -dt * rate, 3)
    r_s[...] = running
    rt = jnp.transpose(running)
    rt_s[...] = rt[0:16, :]
    last = running[255:256, :]
    erx = split_left(jnp.exp(running), expand, 2)
    etx = split_left(jnp.exp(last - running), expand, 2)
    dtx = split_left(dt, expand, 2)
    xv = x_ref[...]
    mask = mask_ref[...]
    dy = (back_ref[...].astype(f32) * mask[:, 0:1]).astype(bf16)
    dy_s[...] = dy
    xs = (xv.astype(f32) * dtx).astype(bf16)
    xs_s[...] = xs
    xe = (xs.astype(f32) * etx).astype(bf16)
    de = (dy.astype(f32) * erx).astype(bf16)

    proj = proj_ref[...]
    inj = [proj[:, 256 * g : 256 * g + 128] for g in range(2)]
    rdo = [proj[:, 256 * g + 128 : 256 * g + 256] for g in range(2)]
    for g in range(2):
        span = slice(512 * g, 512 * g + 512)
        own = dot(xe[:, span], inj[g], ROWS)
        pull = dot(de[:, span], rdo[g], ROWS)
        msg[8 * g : 8 * g + 8, 0:64, :] = own.reshape(8, 64, 128).astype(bf16)
        msg[8 * g : 8 * g + 8, 64:128, :] = pull.reshape(8, 64, 128).astype(bf16)
    decay = jnp.broadcast_to(rt[0:16, 255:256], (16, 128))
    parts = pieces(decay, 3)
    row = iota((16, 16, 128), 1)
    lines = jnp.zeros((16, 16, 128), f32)
    for n, part in enumerate(parts):
        lines = jnp.where(row == n, part.astype(f32)[:, None, :], lines)
    msg[:, 128:144, :] = lines.astype(bf16)

    def to_peer(k):
        to = lax.rem(c + k, 16)
        return remote(msg.at[to], got.at[c], send1.at[k], recv1.at[k], {"ctx": to})

    def from_peer(k):
        who = lax.rem(c + 16 - k, 16)
        return remote(msg.at[who], got.at[who], send1.at[k], recv1.at[k], {"ctx": who})

    def to_peer2(k):
        to = lax.rem(c + k, 16)
        return remote(out.at[to], fin.at[c], send2.at[k], recv2.at[k], {"ctx": to})

    def from_peer2(k):
        who = lax.rem(c + 16 - k, 16)
        return remote(out.at[who], fin.at[who], send2.at[k], recv2.at[k], {"ctx": who})

    def each(fn):
        def body(k, carry):
            fn(k)
            return carry

        lax.fori_loop(1, 16, body, 0)

    each(lambda k: to_peer(k).start())
    for act in acts:
        act.start()
    got[c] = msg[c]

    side = iota((256, 128), 1)

    def group(g):
        bg, cg = inj[g], rdo[g]
        scores = dot(cg, bg, COLS)
        ds_s[g] = jnp.zeros((256, 256), f32)

        def pair(p, carry):
            at_lane = pl.ds(pl.multiple_of(512 * g + p * 128, 128), 128)
            x2 = xs_s[:, at_lane]
            dy2 = dy_s[:, at_lane]
            y2 = jnp.zeros((256, 128), f32)
            z2 = jnp.zeros((256, 128), f32)
            ds = ds_s[g]
            for half in range(2):
                head = 8 * g + 2 * p + half
                col = jnp.sum(jnp.where(side == head, r_s[...], 0.0), axis=1, keepdims=True)
                line = rt_s[pl.ds(head, 1), :]
                grow = jnp.exp(jnp.where(above, col - line, -1e30))
                mine = (side >= 64) if half else (side < 64)
                xm = jnp.where(mine, x2, jnp.zeros_like(x2))
                dm = jnp.where(mine, dy2, jnp.zeros_like(dy2))
                w = (scores * grow).astype(bf16)
                y2 += dot(w, xm)
                z2 += dot(w, dm, ROWS)
                ds += dot(dm, xm, COLS) * grow
            y_s[:, at_lane] = y2
            z_s[:, at_lane] = z2
            ds_s[g] = ds
            return carry

        lax.fori_loop(0, 4, pair, 0)

    group(0)

    each(lambda k: from_peer(k).wait_recv())

    def grow_of(k):
        lines = got[k, 128:144, :].astype(f32)
        return jnp.exp(lines[0:1] + lines[1:2] + lines[2:3])

    def ahead(k, state):
        out[k, 0:64, :] = state.astype(bf16)
        return grow_of(k) * state + got[k, 0:64, :].astype(f32)

    lax.fori_loop(0, 16, ahead, jnp.zeros((64, 128), f32))

    def behind(n, state):
        k = 15 - n
        out[k, 64:128, :] = state.astype(bf16)
        return grow_of(k) * state + got[k, 64:128, :].astype(f32)

    lax.fori_loop(0, 16, behind, jnp.zeros((64, 128), f32))
    each(lambda k: to_peer2(k).start())
    fin[c] = out[c]

    group(1)

    each(lambda k: from_peer2(k).wait_recv())

    skipx = split_left(jnp.broadcast_to(par_ref[1:2, :], (8, 128)), expand, 3)[0:1, :]
    sums_q = jnp.zeros((256, 128), f32)
    sums_v = jnp.zeros((256, 128), f32)
    sums_u = jnp.zeros((256, 128), f32)
    ends = jnp.zeros((8, 128), f32)
    ones = jnp.ones((8, 128), bf16)
    for g in range(2):
        span = slice(512 * g, 512 * g + 512)
        bg, cg = inj[g], rdo[g]
        state = fin[8 * g : 8 * g + 8, 0:64, :].reshape(512, 128)
        later = fin[8 * g : 8 * g + 8, 64:128, :].reshape(512, 128)
        ex = expand[:, span]
        ya = dot(cg, state, COLS) * erx[:, span]
        zs = dot(bg, later, COLS) * etx[:, span]
        dsr = ds_s[g].astype(bf16)
        db = dot(dsr, cg, ROWS) + dot(xe[:, span], later)
        dc = dot(dsr, bg) + dot(de[:, span], state)
        rnd_ref[:, 256 * g : 256 * g + 128] = db.astype(bf16)
        rnd_ref[:, 256 * g + 128 : 256 * g + 256] = dc.astype(bf16)
        xg = xv[:, span].astype(f32)
        xsg = xs[:, span].astype(f32)
        dyg = dy[:, span].astype(f32)
        zw = z_s[:, span]
        yt = y_s[:, span] + ya
        zt = zw + zs
        res_ref[:, span] = (mask[:, 0:1] * (yt + skipx[:, span] * xg)).astype(bf16)
        hg_ref[:, span] = (dtx[:, span] * zt + skipx[:, span] * dyg).astype(bf16)
        sums_q += split_left(dyg * yt - xsg * zw, ex, 3, COLS)
        sums_v += split_left(xsg * zs, ex, 2, COLS)
        sums_u += split_left(xg * zt, ex, 2, COLS)
        rows = split_right(ones, state.astype(f32) * later.astype(f32), 2, COLS)
        ends += split_left(rows, ex, 2, COLS)
    triu = jnp.where(iota((256, 256), 0) <= iota((256, 256), 1), 1.0, 0.0).astype(bf16)
    lower = jnp.where(iota((256, 256), 0) > iota((256, 256), 1), 1.0, 0.0).astype(bf16)
    flow = split_right(triu, sums_q, 3) + split_right(lower, sums_v, 3)
    flow = flow + ends[0:1, :] * jnp.exp(last)
    sg_ref[...] = sig_ref[...] * (sums_u - rate * flow)

    own_up.wait()
    own_lin.wait()
    for n, (src, dst) in enumerate(((up, upq), (lin, linq))):
        for k in (1, 3, 2):
            who = lax.rem(x + 4 - k, 4)
            remote(
                src.at[:, quarter(who)], dst.at[who], send3.at[n, k], recv3.at[n, k], {"dp": who}
            ).wait_recv()
    for act in acts:
        act.wait_send()
    each(lambda k: to_peer(k).wait_send())
    each(lambda k: to_peer2(k).wait_send())


def scan_call(x, dt, sig, mask, par, proj, back, lin, up):
    quarters = jax.ShapeDtypeStruct((4, 256, 512), bf16)
    return pl.pallas_call(
        scan_kernel,
        out_shape=(
            jax.ShapeDtypeStruct((256, 1024), bf16),
            jax.ShapeDtypeStruct((256, 512), bf16),
            jax.ShapeDtypeStruct((256, 1024), bf16),
            jax.ShapeDtypeStruct((256, 128), f32),
            quarters,
            quarters,
        ),
        in_specs=[VM] * 7 + [ANY] * 2,
        out_specs=(VM, VM, VM, VM, ANY, ANY),
        scratch_shapes=[
            pltpu.VMEM((256, 1024), f32),
            pltpu.VMEM((256, 1024), f32),
            pltpu.VMEM((256, 1024), bf16),
            pltpu.VMEM((256, 1024), bf16),
            pltpu.VMEM((2, 256, 256), f32),
            pltpu.VMEM((256, 128), f32),
            pltpu.VMEM((16, 256), f32),
            pltpu.VMEM((16, 144, 128), bf16),
            pltpu.VMEM((16, 144, 128), bf16),
            pltpu.VMEM((16, 128, 128), bf16),
            pltpu.VMEM((16, 128, 128), bf16),
            pltpu.SemaphoreType.DMA((16,)),
            pltpu.SemaphoreType.DMA((16,)),
            pltpu.SemaphoreType.DMA((16,)),
            pltpu.SemaphoreType.DMA((16,)),
            pltpu.SemaphoreType.DMA((2, 4)),
            pltpu.SemaphoreType.DMA((2, 4)),
            pltpu.SemaphoreType.DMA((2,)),
        ],
        compiler_params=pltpu.CompilerParams(
            collective_id=2, has_side_effects=True, vmem_limit_bytes=LIMIT
        ),
        name="scan",
    )(x, dt, sig, mask, par, proj, back, lin, up)


def grads_kernel(
    res, rnd, linq, upq, winj, lg, wg, ig,
    factor, act, w_v, rnd_v, part, half_in, pair_out, pair_in, acc, ring_out, ring_in, y_out, y_in,
    send, recv, zsend, zrecv, ysend, yrecv, tsend, trecv, local,
):
    x, c, t, z, at = places()
    yl = lax.div(c, 8)
    cr = lax.rem(t, 2)
    lefts, rights, opposite = lax.rem(x + 3, 4), lax.rem(x + 1, 4), lax.rem(x + 2, 4)
    source = [res.at[:, 0:512], res.at[:, 512:1024], rnd]
    loads = [
        pltpu.make_async_copy(source[g], factor.at[g, x], local.at[g]) for g in range(3)
    ] + [
        pltpu.make_async_copy(upq, act.at[0], local.at[3]),
        pltpu.make_async_copy(linq, act.at[1], local.at[4]),
        pltpu.make_async_copy(winj, w_v, local.at[5]),
        pltpu.make_async_copy(rnd, rnd_v, local.at[6]),
    ]
    for load in loads:
        load.start()
    greet([at[k] for k in ("right", "left", "up", "down", "across", "core", "far")])
    sent = []

    def go(copy):
        copy.start()
        sent.append(copy)

    def rows(q):
        return pl.ds(q * 128, 128)

    def first(g, q, event, where):
        go(
            remote(
                source[g].at[rows(q)],
                factor.at[g, x, rows(q)],
                send.at[g, event],
                recv.at[g, event],
                where,
            )
        )

    def arrived(g, slab, q, event):
        dst = factor.at[g, slab, rows(q)]
        remote(dst, dst, send.at[g, event], recv.at[g, event], at["left"]).wait_recv()

    def forward(g, slab, q, event, where):
        dst = factor.at[g, slab, rows(q)]
        go(remote(dst, dst, send.at[g, event], recv.at[g, event], where))

    for g in range(3):
        first(g, 0, 0, at["right"])
        first(g, 1, 2, at["left"])
        first(g, 1, 1, at["right"])
        first(g, 0, 3, at["left"])

    def relay(g):
        arrived(g, lefts, 0, 0)
        forward(g, lefts, 0, 4, at["right"])
        arrived(g, rights, 1, 2)
        forward(g, rights, 1, 5, at["left"])

    def product(g):
        arrived(g, lefts, 1, 1)
        arrived(g, rights, 0, 3)
        arrived(g, opposite, 0, 4)
        arrived(g, opposite, 1, 5)
        a = act[0 if g < 2 else 1].reshape(1024, 512)
        acc[g] = dot(a, factor[g].reshape(1024, 512), ROWS).reshape(16, 32, 512)

    def piece(g, d, k):
        lanes = slice(256 * d, 256 * d + 256)
        return acc[g, k, :, lanes], acc[g, 8 + k, :, lanes]

    def ring(g, step):
        for d in range(2):
            k = lax.rem(z + 15 - step, 8) if d == 0 else lax.rem(z + 1 + step, 8)
            low, high = piece(g, d, k)
            if step > 0:
                came = ring_in.at[g, d, step - 1]
                remote(
                    came, came, zsend.at[g, d, step - 1], zrecv.at[g, d, step - 1], at["up"]
                ).wait_recv()
                low += came[0].astype(f32)
                high += came[1].astype(f32)
            if step < 7:
                ring_out[g, d, step, 0] = low.astype(bf16)
                ring_out[g, d, step, 1] = high.astype(bf16)
                go(
                    remote(
                        ring_out.at[g, d, step],
                        ring_in.at[g, d, step],
                        zsend.at[g, d, step],
                        zrecv.at[g, d, step],
                        at["up"] if d == 0 else at["down"],
                    )
                )
            else:
                lanes = slice(256 * d, 256 * d + 256)
                acc[g, z, :, lanes] = low
                acc[g, 8 + z, :, lanes] = high
        if step == 7:
            y_out[g] = acc[g, (1 - yl) * 8 + z].astype(bf16)
            go(
                remote(y_out.at[g], y_in.at[g], ysend.at[g], yrecv.at[g], at["across"])
            )

    def finish(g):
        remote(y_out.at[g], y_in.at[g], ysend.at[g], yrecv.at[g], at["across"]).wait_recv()
        total = acc[g, c] + y_in[g].astype(f32)
        if g < 2:
            wg[:, 512 * g : 512 * g + 512] = total
        else:
            ig[...] = total

    mine = pl.ds(pl.multiple_of(cr * 128, 128), 128)
    other = pl.ds(pl.multiple_of((1 - cr) * 128, 128), 128)
    loads[5].wait()
    loads[6].wait()
    part[...] = dot(rnd_v[...], w_v[...], COLS)
    half_in[1] = part[other, :].astype(bf16)
    go(remote(half_in.at[1], half_in.at[0], tsend.at[0], trecv.at[0], at["core"]))
    for load in loads[:5]:
        load.wait()
    relay(0)
    remote(half_in.at[1], half_in.at[0], tsend.at[0], trecv.at[0], at["core"]).wait_recv()
    pair_out[...] = (part[mine, :] + half_in[0].astype(f32)).astype(bf16)
    go(remote(pair_out, pair_in, tsend.at[1], trecv.at[1], at["far"]))
    relay(1)
    product(0)
    ring(0, 0)
    ring(0, 1)
    relay(2)
    ring(0, 2)
    product(1)
    ring(0, 3)
    ring(1, 0)
    ring(0, 4)
    ring(1, 1)
    ring(0, 5)
    ring(1, 2)
    product(2)
    ring(0, 6)
    ring(1, 3)
    ring(2, 0)
    remote(pair_out, pair_in, tsend.at[1], trecv.at[1], at["far"]).wait_recv()
    lg[mine, :] = (pair_out[...].astype(f32) + pair_in[...].astype(f32)).astype(bf16)
    go(remote(lg.at[mine], lg.at[mine], tsend.at[2], trecv.at[2], at["core"]))
    ring(0, 7)
    ring(1, 4)
    ring(2, 1)
    ring(1, 5)
    ring(2, 2)
    ring(1, 6)
    ring(2, 3)
    ring(1, 7)
    ring(2, 4)
    finish(0)
    ring(2, 5)
    ring(2, 6)
    finish(1)
    ring(2, 7)
    finish(2)
    remote(lg.at[other], lg.at[other], tsend.at[2], trecv.at[2], at["core"]).wait_recv()
    for s in sent:
        s.wait_send()


def grads_call(res, rnd, linq, upq, winj):
    return pl.pallas_call(
        grads_kernel,
        out_shape=(
            jax.ShapeDtypeStruct((256, 2048), bf16),
            jax.ShapeDtypeStruct((32, 1024), f32),
            jax.ShapeDtypeStruct((32, 512), f32),
        ),
        in_specs=[ANY] * 5,
        out_specs=(VM, VM, VM),
        scratch_shapes=[
            pltpu.VMEM((3, 4, 256, 512), bf16),
            pltpu.VMEM((2, 4, 256, 512), bf16),
            pltpu.VMEM((2048, 512), bf16),
            pltpu.VMEM((256, 512), bf16),
            pltpu.VMEM((256, 2048), f32),
            pltpu.VMEM((2, 128, 2048), bf16),
            pltpu.VMEM((128, 2048), bf16),
            pltpu.VMEM((128, 2048), bf16),
            pltpu.VMEM((3, 16, 32, 512), f32),
            pltpu.VMEM((3, 2, 7, 2, 32, 256), bf16),
            pltpu.VMEM((3, 2, 7, 2, 32, 256), bf16),
            pltpu.VMEM((3, 32, 512), bf16),
            pltpu.VMEM((3, 32, 512), bf16),
            pltpu.SemaphoreType.DMA((3, 6)),
            pltpu.SemaphoreType.DMA((3, 6)),
            pltpu.SemaphoreType.DMA((3, 2, 7)),
            pltpu.SemaphoreType.DMA((3, 2, 7)),
            pltpu.SemaphoreType.DMA((3,)),
            pltpu.SemaphoreType.DMA((3,)),
            pltpu.SemaphoreType.DMA((3,)),
            pltpu.SemaphoreType.DMA((3,)),
            pltpu.SemaphoreType.DMA((7,)),
        ],
        compiler_params=pltpu.CompilerParams(
            collective_id=3, has_side_effects=True, vmem_limit_bytes=LIMIT
        ),
        name="grads",
    )(res, rnd, linq, upq, winj)


def per_device(
    layer_in, head_in, step_raw, step_bias, rate_log, skip_gain,
    inject_weight, out_weight, upstream, window_start, lengths,
):
    tokens = head_in.shape[1]
    inputs, incoming = layer_in[0], upstream[0]
    wi = inject_weight.reshape(512, 512)
    positions = lax.axis_index("ctx") * tokens + jnp.arange(tokens, dtype=jnp.int32)
    mask = ((positions >= window_start[0]) & (positions < lengths[0])).astype(f32)[:, None]
    shifted = step_raw[0] + step_bias
    wide = ((0, 0), (0, 112))
    dt = jnp.pad(mask * jax.nn.softplus(shifted), wide)
    sig = jnp.pad(mask * jax.nn.sigmoid(shifted), wide)
    par = jnp.pad(jnp.stack([jnp.exp(rate_log), skip_gain]), ((0, 6), (0, 112)))
    masks = jnp.broadcast_to(mask, (tokens, 128))
    proj, back, winj = weights_call(wi, out_weight, inputs, incoming)
    res, rnd, hg, sg, linq, upq = scan_call(
        head_in[0], dt, sig, masks, par, proj, back, inputs, incoming
    )
    lg, wg, ig = grads_call(res, rnd, linq, upq, winj)
    return lg[None], hg[None], sg[None, :, :16], wg, ig.reshape(32, 2, 256)


def solution(mesh):
    placed = (
        P("dp", "ctx", None),
        P("dp", "ctx", "tensor"),
        P("dp", "ctx", "tensor"),
        P("tensor"),
        P("tensor"),
        P("tensor"),
        P("dp", "tensor", None),
        P("dp", "tensor"),
        P("dp", "ctx", None),
        P("dp"),
        P("dp"),
    )
    return jax.shard_map(
        per_device,
        mesh=mesh,
        in_specs=placed,
        out_specs=(
            P("dp", "ctx", None),
            P("dp", "ctx", "tensor"),
            P("dp", "ctx", "tensor"),
            P(("dp", "ctx"), "tensor"),
            P(("dp", "ctx"), "tensor", None),
        ),
        check_vma=False,
    )
```

time: 1310 us -> 175 us (0.13)
  waiting for transfers between devices: 1040 us -> 0 us
  Pallas kernels: 0 us -> 157 us
  blocking collectives: 85.4 us -> 0 us
  local copies, waits for them, and re-layouts: 67.4 us -> 11.5 us
  matrix products: 48.5 us -> 0 us
  other arithmetic: 50.5 us -> 2.03 us
  between operations: 16.7 us -> 1.99 us
    unnamed x8 -> x0, waiting for transfers between devices: 855 us -> none
    all_gather x4 -> x0, waiting for transfers between devices: 185 us -> none  [the longest x2 107 us: entering_2(): everything = jax.tree.map(lambda part: lax.all_gather(part, axis), x)]
    pallas_call x0 -> x3, Pallas kernels: none -> 157 us  [the longest x1 75.6 us: grads_call(): pl.pallas_call(grads_kernel, out_shape=(jax.ShapeDtypeStruct((256, 2048),...]
    psum x1 -> x0, blocking collectives: 49.7 us -> none  [per_device(): layer_grad = lax.psum(partial_value, 'tensor').astype(jnp.bfloat16)]
    dot_general x19 -> x0, matrix products: 48.5 us -> none  [the longest x3 12.5 us: block_parts(): jnp.einsum('ctsgj,csgjp->ctgjp', weighted, head_values, precision=highest)]
    select_n x32 -> x0, other arithmetic: 37.6 us -> none  [hop(): return jax.tree.map(lambda a, b: jnp.where(reached, a, b), new, before)]
    all_gather x1 -> x0, blocking collectives: 35.7 us -> none  [entering_2(): everything = jax.tree.map(lambda part: lax.all_gather(part, axis), x)]
    exp x33 -> x0, local copies, waits for them, and re-layouts: 21.3 us -> none  [the longest x32 21.3 us: chain_step(): jnp.exp(later[0])[..., None, None] * earlier[1] + later[1]]
  transfers between devices with their start and end apart: 6 -> 0, of which waited for: 6 -> 0; matrix products, arithmetic and copies ran while one was open for 9% -> 0% of each run, Pallas kernels for 0% -> 0%
where the time goes in v1:
time: 175 us; the launch traced here: 173 us
  Pallas kernels  157 us (90%)
  local copies, waits for them, and re-layouts  11.5 us (7%)
  other arithmetic  2.03 us (1%)
  between operations  1.99 us (1%)
    pallas_call x1, Pallas kernels, grads_call(): pl.pallas_call(grads_kernel, out_shape=(jax.ShapeDtypeStruct((256, 2048),...  75.6 us
    pallas_call x1, Pallas kernels, weights_call(): pl.pallas_call(weights_kernel, out_shape=(jax.ShapeDtypeStruct((256, 512)...  43.7 us
    pallas_call x1, Pallas kernels, scan_call(): pl.pallas_call(scan_kernel, out_shape=(jax.ShapeDtypeStruct((256, 1024),...  38.2 us
    unnamed x12, local copies, waits for them, and re-layouts  7.18 us

profile of v1, /device:TPU:16, one launch (start us, length us, event | category | flops | bytes accessed | tf_op | source)
XLA Modules:
  0.0 173.0 jit_solution(9182743535422931696)
XLA Ops:
  1.9 0.7 exponential_bitcast_fusion
  2.6 1.3 select_maximum_fusion.par_ref
  3.9 0.8 copy.18
  4.7 0.8 broadcast_in_dim.16.mask_ref
  5.4 0.8 divide_multiply_fusion
  6.2 0.7 pad.12.sig_ref
  6.9 0.7 pad.11.dt_ref
  7.5 1.9 %copy.22 = bf16[64,8,2,256]{3,1,2,0:T(8,128)(2,1)} copy(bf16[64,8,2,256]{3,2,1,0:T(2,128)(2,1)} %bitcast.28) | data formatting | bytes 1048576
  9.5 43.7 %weights.1 = (bf16[256,512]{1,0:T(8,128)(2,1)}, bf16[256,1024]{1,0:T(8,128)(2,1)}, bf16[2048,512]{1,0:T(8,128)(2,1)}) custom-call(bf16[512,512]{1,0:T(8,128)(2,1)} %bitcast.26, bf16[512,1024]{1,0:T(8,128)(2,1)} %wo.1, bf16[256,2048]{1,0:T(8,128)(2,1)} %bitcast.22, bf16[256,2048]{1,0:T(8,128)(2,1)} %bitcast.24), custom_call_target="tpu_custom_call" | custom-call | tf_op jit(solution)/shard_map/weights/pallas_call | solution.py:156
  53.1 38.2 %scan.1 = (bf16[256,1024]{1,0:T(8,128)(2,1)}, bf16[256,512]{1,0:T(8,128)(2,1)}, bf16[256,1024]{1,0:T(8,128)(2,1)}, f32[256,128]{1,0:T(8,128)}, bf16[4,256,512]{2...) custom-call(bf16[256,1024]{1,0:T(8,128)(2,1)} %bitcast.30, f32[256,128]{1,0:T(8,128)} %pad.11.dt_ref, f32[256,128]{1,0:T(8,128)} %pad.12.sig_ref, ...), custom_call_target="tpu_custom_call" | custom-call | tf_op jit(solution)/shard_map/scan/pallas_call | solution.py:398
  91.3 0.0 copy-start.1
  91.3 75.6 %grads.1 = (bf16[256,2048]{1,0:T(8,128)(2,1)}, f32[32,1024]{1,0:T(8,128)}, f32[32,512]{1,0:T(8,128)}) custom-call(bf16[256,1024]{1,0:T(8,128)(2,1)} %get-tuple-element.19.res, bf16[256,512]{1,0:T(8,128)(2,1)} %get-tuple-element.20.rnd, bf16[4,256,512]{2,1,0:T(8,128)(2,1)} %get-tuple-element.21.linq, bf16[4,256,512]{2,1,0:T(8,128)(2,1)} %get-tuple-element.22.upq, ...), custom_call_target="tpu_custom_call" | custom-call | tf_op jit(solution)/shard_map/grads/pallas_call | solution.py:605
  167.0 0.0 copy-start
  167.0 0.0 copy-start.2
  167.0 1.6 reshape.26
  168.6 0.0 copy-done.1
  168.6 0.7 copy.21
  169.3 2.3 %copy.28 = bf16[1,256,2048]{2,1,0:T(8,128)(2,1)} copy(bf16[1,256,2048]{2,1,0:T(8,128)(2,1)} %bitcast.27) | data formatting | bytes 2097152
  171.6 0.0 copy-done
  171.6 0.8 copy.29
  172.4 0.0 copy-done.2
  172.4 0.7 copy.30
  (2 shorter events, 0.0 us)
Async XLA Ops:
  91.3 77.2 %copy-start.1 = (f32[256,128]{1,0:T(8,128)S(1)}, f32[256,128]{1,0:T(8,128)}, u32[]{:S(2)}) copy-start(f32[256,128]{1,0:T(8,128)} %get-tuple-element.26) | copy-start | bytes 393220
  167.0 4.6 %copy-start = (bf16[256,1024]{1,0:T(8,128)(2,1)S(1)}, bf16[256,1024]{1,0:T(8,128)(2,1)}, u32[]{:S(2)}) copy-start(bf16[256,1024]{1,0:T(8,128)(2,1)} %get-tuple-element.25) | copy-start | bytes 1572868
  167.0 5.4 %copy-start.2 = (f32[32,1024]{1,0:T(8,128)S(1)}, f32[32,1024]{1,0:T(8,128)}, u32[]{:S(2)}) copy-start(f32[32,1024]{1,0:T(8,128)} %get-tuple-element.49) | copy-start | bytes 393220

commit v2 on v0

v2 whole, which is shorter than its diff:
```python
import jax
import jax.numpy as jnp
from jax import lax
from jax.experimental import pallas as pl
from jax.experimental.pallas import tpu as pltpu
from jax.sharding import PartitionSpec as P

f32 = jnp.float32
bf16 = jnp.bfloat16
MESH = pl.DeviceIdType.MESH
ANY = pl.BlockSpec(memory_space=pl.ANY)
VM = pl.BlockSpec(memory_space=pltpu.VMEM)
WINDOW = 2
LIMIT = 56 * 1024 * 1024
ROWS = (((0,), (0,)), ((), ()))
COLS = (((1,), (1,)), ((), ()))


def remote(src, dst, send, recv, where):
    return pltpu.make_async_remote_copy(
        src_ref=src, dst_ref=dst, send_sem=send, recv_sem=recv, device_id=where, device_id_type=MESH
    )


def greet(partners):
    barrier = pltpu.get_barrier_semaphore()
    for where in partners:
        pl.semaphore_signal(barrier, inc=1, device_id=where, device_id_type=MESH)
    pl.semaphore_wait(barrier, len(partners))


def places():
    x = lax.axis_index("dp")
    c = lax.axis_index("ctx")
    t = lax.axis_index("tensor")
    z = lax.rem(c, 8)
    base = c - z
    spots = dict(
        right={"dp": lax.rem(x + 1, 4)},
        left={"dp": lax.rem(x + 3, 4)},
        up={"ctx": base + lax.rem(z + 1, 8)},
        down={"ctx": base + lax.rem(z + 7, 8)},
        across={"ctx": lax.rem(c + 8, 16)},
        core={"tensor": t + 1 - 2 * lax.rem(t, 2)},
        far={"tensor": lax.rem(t + 2, 4)},
    )
    return x, c, t, z, spots


def dot(a, b, dims=None):
    if dims is None:
        return jnp.dot(a, b, preferred_element_type=f32)
    return lax.dot_general(a, b, dims, preferred_element_type=f32)


def pieces(v, count):
    found = []
    for _ in range(count):
        part = v.astype(bf16)
        found.append(part)
        v = v - part.astype(f32)
    return found


def split_left(v, m, count, dims=None):
    return sum(dot(part, m, dims) for part in pieces(v, count))


def split_right(m, v, count, dims=None):
    return sum(dot(m, part, dims) for part in pieces(v, count))


def iota(shape, axis):
    return lax.broadcasted_iota(jnp.int32, shape, axis)


class Lane:
    def __init__(self, window):
        self.window = window
        self.sent = []
        self.waited = 0

    def push(self, copy):
        while len(self.sent) - self.waited >= self.window:
            self.sent[self.waited].wait_send()
            self.waited += 1
        copy.start()
        self.sent.append(copy)

    def drain(self):
        while self.waited < len(self.sent):
            self.sent[self.waited].wait_send()
            self.waited += 1


def kernel(
    x_ref, raw_ref, bias_ref, rate_ref, skip_ref, start_ref, stop_ref, wi, wo, lin, up,
    lg, hg_ref, sg_ref, wg, ig,
    wi_v, wo_v, lin_v, up_v, proj_s, back_s, y_s, z_s, xs_s, xe_s, dy_s, de_s, erx_s, etx_s, dtx_s, ds_s,
    r_s, rt_s, f_out, f_got, f_mid, f_fin, b_out, b_got, b_mid, b_fin,
    factor, act, part, half_out, half_in, pair_out, pair_in, acc, ring_out, ring_in, y_out, y_in,
    wsend, wrecv, asend, arecv, csend, crecv, esend, erecv,
    send, recv, zsend, zrecv, ysend, yrecv, tsend, trecv, local,
):
    x, c, t, z, at = places()
    h = lax.rem(z, 2)
    yl = lax.div(c, 8)
    cr = lax.rem(t, 2)
    lefts, rights, opposite = lax.rem(x + 3, 4), lax.rem(x + 1, 4), lax.rem(x + 2, 4)
    mine = pl.ds(pl.multiple_of(cr * 128, 128), 128)
    other = pl.ds(pl.multiple_of((1 - cr) * 128, 128), 128)

    def quarter(j):
        return pl.ds(pl.multiple_of(j * 512, 512), 512)

    loads = [
        pltpu.make_async_copy(wi, wi_v.at[quarter(x)], local.at[0]),
        pltpu.make_async_copy(wo, wo_v.at[quarter(x)], local.at[1]),
        pltpu.make_async_copy(lin, lin_v, local.at[2]),
        pltpu.make_async_copy(up, up_v, local.at[3]),
    ]
    for load in loads:
        load.start()
    greet(
        [at[k] for k in ("right", "left", "core", "far")]
        + [{"dp": opposite}]
        + [{"ctx": lax.rem(c + k, 16)} for k in range(1, 16)]
    )

    links = {k: Lane(WINDOW) for k in ("right", "left", "up", "down")}

    def strip(ref, g):
        return ref if g == 0 else ref.at[:, 512 * (g - 1) : 512 * g]

    def weight_rows(g, slab, half, q):
        rows = pl.ds(pl.multiple_of(slab * 512 + half * 256 + q * 128, 128), 128)
        return strip(wi_v if g == 0 else wo_v, g).at[rows]

    def first(g, q, event, way):
        rows = pl.ds(pl.multiple_of(h * 256 + q * 128, 128), 128)
        links[way].push(
            remote(
                strip(wi if g == 0 else wo, g).at[rows],
                weight_rows(g, x, h, q),
                wsend.at[g, event],
                wrecv.at[g, event],
                at[way],
            )
        )

    def arrived(g, slab, half, q, event):
        dst = weight_rows(g, slab, half, q)
        remote(dst, dst, wsend.at[g, event], wrecv.at[g, event], at["left"]).wait_recv()

    def forward(g, slab, q, event, way):
        dst = weight_rows(g, slab, h, q)
        links[way].push(remote(dst, dst, wsend.at[g, event], wrecv.at[g, event], at[way]))

    def slot(g, n):
        if n == 0:
            first(g, 0, 0, "right")
            first(g, 1, 2, "left")
        elif n == 1:
            first(g, 1, 1, "right")
            first(g, 0, 3, "left")
        elif n == 2:
            arrived(g, lefts, h, 0, 0)
            forward(g, lefts, 0, 4, "right")
            arrived(g, rights, h, 1, 2)
            forward(g, rights, 1, 5, "left")
            forward(g, lefts, 0, 6, "up")
            forward(g, rights, 1, 10, "down")
        elif n == 3:
            arrived(g, lefts, h, 1, 1)
            forward(g, lefts, 1, 9, "down")
            arrived(g, rights, h, 0, 3)
            forward(g, rights, 0, 7, "up")
        else:
            arrived(g, opposite, h, 0, 4)
            forward(g, opposite, 0, 8, "up")
            arrived(g, opposite, h, 1, 5)
            forward(g, opposite, 1, 11, "down")

    def gathered(g):
        for n, slab in enumerate((lefts, rights, opposite)):
            arrived(g, slab, 1 - h, 0, 6 + n)
            arrived(g, slab, 1 - h, 1, 9 + n)

    def swap(e, src, dst):
        def to_peer(k):
            to = lax.rem(c + k, 16)
            return remote(src.at[to], dst.at[c], esend.at[e, k], erecv.at[e, k], {"ctx": to})

        def from_peer(k):
            who = lax.rem(c + 16 - k, 16)
            return remote(src.at[who], dst.at[who], esend.at[e, k], erecv.at[e, k], {"ctx": who})

        def each(fn):
            def step(k, carry):
                fn(k)
                return carry

            lax.fori_loop(1, 16, step, 0)

        def begin():
            each(lambda k: to_peer(k).start())
            dst[c] = src[c]

        return (
            begin,
            lambda: each(lambda k: from_peer(k).wait_recv()),
            lambda: each(lambda k: to_peer(k).wait_send()),
        )

    f1 = swap(0, f_out, f_got)
    f2 = swap(1, f_mid, f_fin)
    b1 = swap(2, b_out, b_got)
    b2 = swap(3, b_mid, b_fin)

    slot(0, 0)
    slot(0, 1)

    side16 = iota((16, 1024), 1) - 64 * iota((16, 1024), 0)
    expand = jnp.where((side16 >= 0) & (side16 < 64), 1.0, 0.0).astype(bf16)
    above = iota((256, 256), 0) >= iota((256, 256), 1)
    tril = jnp.where(above, 1.0, 0.0).astype(bf16)
    eye = jnp.where(iota((256, 256), 0) == iota((256, 256), 1), 1.0, 0.0).astype(bf16)
    position = c * 256 + iota((256, 1), 0)
    mask = jnp.where((position >= start_ref[...]) & (position < stop_ref[...]), 1.0, 0.0)
    rate = jnp.exp(rate_ref[...])
    shifted = raw_ref[...] + bias_ref[...]
    small = jnp.exp(-jnp.abs(shifted))
    dt = mask * (jnp.maximum(shifted, 0.0) + jnp.log1p(small))
    sig = mask * jnp.where(shifted >= 0.0, 1.0, small) / (1.0 + small)
    running = split_right(tril, -dt * rate, 3)
    r_s[...] = running
    rt = split_left(running, eye, 3, ROWS)
    rt_s[...] = rt
    last = running[255:256, :]
    erx_s[...] = split_left(jnp.exp(running), expand, 2)
    etx_s[...] = split_left(jnp.exp(last - running), expand, 2)
    dtx_s[...] = split_left(dt, expand, 2)
    xs_s[...] = (x_ref[...].astype(f32) * dtx_s[...]).astype(bf16)
    xe_s[...] = (xs_s[...].astype(f32) * etx_s[...]).astype(bf16)
    skipx = split_left(jnp.broadcast_to(skip_ref[...], (8, 16)), expand, 3)[0:1, :]
    decay = jnp.broadcast_to(rt[:, 255:256], (16, 128))
    row = iota((16, 16, 128), 1)
    lines = jnp.zeros((16, 16, 128), f32)
    for n, term in enumerate(pieces(decay, 3)):
        lines = jnp.where(row == n, term.astype(f32)[:, None, :], lines)
    f_out[:, 64:80, :] = lines.astype(bf16)

    slot(0, 2)
    slot(1, 0)
    slot(0, 3)
    slot(1, 1)
    slot(0, 4)
    for load in loads:
        load.wait()
    gathered(0)

    def spans(g):
        return slice(512 * g, 512 * g + 512)

    def bs(g):
        return proj_s[:, 256 * g : 256 * g + 128]

    def cs(g):
        return proj_s[:, 256 * g + 128 : 256 * g + 256]

    proj_s[...] = dot(lin_v[...], wi_v[...]).astype(bf16)
    for g in range(2):
        own = dot(xe_s[:, spans(g)], bs(g), ROWS)
        f_out[8 * g : 8 * g + 8, 0:64, :] = own.reshape(8, 64, 128).astype(bf16)
    f1[0]()
    slot(1, 2)
    slot(2, 0)
    slot(1, 3)
    slot(2, 1)
    slot(1, 4)
    slot(2, 2)

    def grow_of(k):
        lines = f_got[k, 64:80, :].astype(f32)
        return jnp.exp(lines[0:1] + lines[1:2] + lines[2:3])

    f1[1]()

    def ahead(k, state):
        f_mid[k] = state.astype(bf16)
        return grow_of(k) * state + f_got[k, 0:64, :].astype(f32)

    lax.fori_loop(0, 16, ahead, jnp.zeros((64, 128), f32))
    f2[0]()
    slot(2, 3)
    slot(2, 4)

    values = (up_v, lin_v)
    acts = []

    def act_send(n):
        for k in (1, 3, 2):
            to = lax.rem(x + k, 4)
            copy = remote(
                values[n].at[mine, quarter(to)],
                act.at[n, x, mine],
                asend.at[n, k],
                arecv.at[n, k],
                {"dp": to},
            )
            copy.start()
            acts.append(copy)
        act[n, x] = values[n][:, quarter(x)]

    def act_share(n):
        for k in (1, 3, 2):
            dst = act.at[n, lax.rem(x + 4 - k, 4), mine]
            remote(dst, dst, asend.at[n, k], arecv.at[n, k], at["left"]).wait_recv()
            copy = remote(dst, dst, csend.at[n, k], crecv.at[n, k], at["core"])
            copy.start()
            acts.append(copy)

    def act_done(n):
        for k in (1, 3, 2):
            dst = act.at[n, lax.rem(x + 4 - k, 4), other]
            remote(dst, dst, csend.at[n, k], crecv.at[n, k], at["core"]).wait_recv()

    act_send(0)
    gathered(1)
    gathered(2)
    act_send(1)
    back = dot(up_v[...], wo_v[...]).astype(bf16).astype(f32)
    dy_s[...] = (back * mask).astype(bf16)
    de_s[...] = (dy_s[...].astype(f32) * erx_s[...]).astype(bf16)
    for g in range(2):
        pull = dot(de_s[:, spans(g)], cs(g), ROWS)
        b_out[8 * g : 8 * g + 8] = pull.reshape(8, 64, 128).astype(bf16)
    b1[0]()

    side = iota((256, 128), 1)
    side16 = iota((256, 16), 1)

    def group(g):
        bg, cg = bs(g), cs(g)
        scores = dot(cg, bg, COLS)
        ds_s[g] = jnp.zeros((256, 256), f32)

        def pair(p, carry):
            lanes = pl.ds(pl.multiple_of(512 * g + p * 128, 128), 128)
            x2 = xs_s[:, lanes]
            dy2 = dy_s[:, lanes]
            y2 = jnp.zeros((256, 128), f32)
            z2 = jnp.zeros((256, 128), f32)
            ds = ds_s[g]
            for half in range(2):
                head = 8 * g + 2 * p + half
                col = jnp.sum(jnp.where(side16 == head, r_s[...], 0.0), axis=1, keepdims=True)
                line = rt_s[pl.ds(head, 1), :]
                grow = jnp.exp(jnp.where(above, col - line, -1e30))
                here = (side >= 64) if half else (side < 64)
                xm = jnp.where(here, x2, jnp.zeros_like(x2))
                dm = jnp.where(here, dy2, jnp.zeros_like(dy2))
                w = (scores * grow).astype(bf16)
                y2 += dot(w, xm)
                z2 += dot(w, dm, ROWS)
                ds += dot(dm, xm, COLS) * grow
            y_s[:, lanes] = y2
            z_s[:, lanes] = z2
            ds_s[g] = ds
            return carry

        lax.fori_loop(0, 4, pair, 0)

    group(0)
    group(1)

    def states(fin, g):
        return fin[8 * g : 8 * g + 8].reshape(512, 128)

    sent = []

    def go(copy):
        copy.start()
        sent.append(copy)

    def own_send(g):
        rows = [pl.ds(0, 128), pl.ds(128, 128)]
        for q, event, way in ((0, 0, "right"), (1, 2, "left"), (1, 1, "right"), (0, 3, "left")):
            src = factor.at[g, x, rows[q]]
            go(remote(src, src, send.at[g, event], recv.at[g, event], at[way]))

    def came(g, slab, q, event):
        dst = factor.at[g, slab, pl.ds(128 * q, 128)]
        remote(dst, dst, send.at[g, event], recv.at[g, event], at["left"]).wait_recv()
        return dst

    def relay(g):
        src = came(g, lefts, 0, 0)
        go(remote(src, src, send.at[g, 4], recv.at[g, 4], at["right"]))
        src = came(g, rights, 1, 2)
        go(remote(src, src, send.at[g, 5], recv.at[g, 5], at["left"]))

    f2[1]()
    for g in range(2):
        span = spans(g)
        ya = dot(cs(g), states(f_fin, g), COLS) * erx_s[:, span]
        yt = y_s[:, span] + ya
        y_s[:, span] = yt
        value = mask * (yt + skipx[:, span] * x_ref[:, span].astype(f32))
        factor[g, x] = value.astype(bf16)
        own_send(g)

    b1[1]()

    def behind(n, state):
        k = 15 - n
        b_mid[k] = state.astype(bf16)
        return grow_of(k) * state + b_got[k].astype(f32)

    lax.fori_loop(0, 16, behind, jnp.zeros((64, 128), f32))
    b2[0]()
    act_share(0)
    relay(0)
    relay(1)
    act_share(1)
    b2[1]()

    for g in range(2):
        later = states(b_fin, g)
        state = states(f_fin, g)
        dsr = ds_s[g].astype(bf16)
        db = dot(dsr, cs(g), ROWS) + dot(xe_s[:, spans(g)], later)
        dc = dot(dsr, bs(g)) + dot(de_s[:, spans(g)], state)
        factor[2, x, :, 256 * g : 256 * g + 128] = db.astype(bf16)
        factor[2, x, :, 256 * g + 128 : 256 * g + 256] = dc.astype(bf16)
    own_send(2)
    part[...] = dot(factor[2, x], wi_v[...], COLS)
    half_out[...] = part[other, :].astype(bf16)
    go(remote(half_out, half_in, tsend.at[0], trecv.at[0], at["core"]))

    def product(g):
        came(g, lefts, 1, 1)
        came(g, rights, 0, 3)
        came(g, opposite, 0, 4)
        came(g, opposite, 1, 5)
        a = act[0 if g < 2 else 1].reshape(1024, 512)
        acc[g] = dot(a, factor[g].reshape(1024, 512), ROWS).reshape(16, 32, 512)

    def pass_on(g, k, slot_in, slot_out, way):
        low, high = acc[g, k], acc[g, 8 + k]
        if slot_in is not None:
            got = ring_in.at[g, slot_in]
            remote(got, got, zsend.at[g, slot_in], zrecv.at[g, slot_in], at["up"]).wait_recv()
            low += got[0].astype(f32)
            high += got[1].astype(f32)
        ring_out[g, slot_out, 0] = low.astype(bf16)
        ring_out[g, slot_out, 1] = high.astype(bf16)
        go(
            remote(
                ring_out.at[g, slot_out],
                ring_in.at[g, slot_out],
                zsend.at[g, slot_out],
                zrecv.at[g, slot_out],
                at[way],
            )
        )

    def ring(g, s):
        if s < 4:
            pass_on(g, lax.rem(z + 4 - s, 8), s - 1 if s else None, s, "up")
        if s < 3:
            pass_on(g, lax.rem(z + 5 + s, 8), s + 3 if s else None, s + 4, "down")
        if s == 4:
            low, high = acc[g, z], acc[g, 8 + z]
            for n in (3, 6):
                got = ring_in.at[g, n]
                remote(got, got, zsend.at[g, n], zrecv.at[g, n], at["up"]).wait_recv()
                low += got[0].astype(f32)
                high += got[1].astype(f32)
            acc[g, z] = low
            acc[g, 8 + z] = high
            y_out[g] = acc[g, (1 - yl) * 8 + z].astype(bf16)
            go(remote(y_out.at[g], y_in.at[g], ysend.at[g], yrecv.at[g], at["across"]))

    def finish(g):
        remote(y_out.at[g], y_in.at[g], ysend.at[g], yrecv.at[g], at["across"]).wait_recv()
        total = acc[g, c] + y_in[g].astype(f32)
        if g < 2:
            wg[:, 512 * g : 512 * g + 512] = total
        else:
            ig[...] = total

    act_done(0)
    product(0)
    ring(0, 0)
    relay(2)
    product(1)
    ring(1, 0)
    ring(0, 1)
    ring(1, 1)
    remote(half_out, half_in, tsend.at[0], trecv.at[0], at["core"]).wait_recv()
    pair_out[...] = (part[mine, :] + half_in[...].astype(f32)).astype(bf16)
    go(remote(pair_out, pair_in, tsend.at[1], trecv.at[1], at["far"]))
    ring(0, 2)
    ring(1, 2)

    sums_q = jnp.zeros((256, 16), f32)
    sums_v = jnp.zeros((256, 16), f32)
    sums_u = jnp.zeros((256, 16), f32)
    ends = jnp.zeros((8, 16), f32)
    ones = jnp.ones((8, 128), bf16)
    for g in range(2):
        span = spans(g)
        later, state = states(b_fin, g), states(f_fin, g)
        ex = expand[:, span]
        zs = dot(bs(g), later, COLS) * etx_s[:, span]
        xg = x_ref[:, span].astype(f32)
        xsg = xs_s[:, span].astype(f32)
        dyg = dy_s[:, span].astype(f32)
        zw = z_s[:, span]
        zt = zw + zs
        hg_ref[:, span] = (dtx_s[:, span] * zt + skipx[:, span] * dyg).astype(bf16)
        sums_q += split_left(dyg * y_s[:, span] - xsg * zw, ex, 3, COLS)
        sums_v += split_left(xsg * zs, ex, 2, COLS)
        sums_u += split_left(xg * zt, ex, 2, COLS)
        rows = split_right(ones, state.astype(f32) * later.astype(f32), 2, COLS)
        ends += split_left(rows, ex, 2, COLS)
    triu = jnp.where(iota((256, 256), 0) <= iota((256, 256), 1), 1.0, 0.0).astype(bf16)
    lower = jnp.where(iota((256, 256), 0) > iota((256, 256), 1), 1.0, 0.0).astype(bf16)
    flow = split_right(triu, sums_q, 3) + split_right(lower, sums_v, 3)
    flow = flow + ends[0:1, :] * jnp.exp(last)
    sg_ref[...] = sig * (sums_u - rate * flow)

    act_done(1)
    product(2)
    ring(2, 0)
    ring(0, 3)
    ring(1, 3)
    ring(2, 1)
    remote(pair_out, pair_in, tsend.at[1], trecv.at[1], at["far"]).wait_recv()
    lg[mine, :] = (pair_out[...].astype(f32) + pair_in[...].astype(f32)).astype(bf16)
    go(remote(lg.at[mine], lg.at[mine], tsend.at[2], trecv.at[2], at["core"]))
    ring(2, 2)
    ring(0, 4)
    ring(1, 4)
    ring(2, 3)
    finish(0)
    finish(1)
    ring(2, 4)
    for lane in links.values():
        lane.drain()
    for copy in acts:
        copy.wait_send()
    for e in (f1, f2, b1, b2):
        e[2]()
    finish(2)
    remote(lg.at[other], lg.at[other], tsend.at[2], trecv.at[2], at["core"]).wait_recv()
    for copy in sent:
        copy.wait_send()


def call(x, raw, bias, rate, skip, start, stop, wi, wo, lin, up):
    def vm(shape, kind=bf16):
        return pltpu.VMEM(shape, kind)

    dma = pltpu.SemaphoreType.DMA
    return pl.pallas_call(
        kernel,
        out_shape=(
            jax.ShapeDtypeStruct((256, 2048), bf16),
            jax.ShapeDtypeStruct((256, 1024), bf16),
            jax.ShapeDtypeStruct((256, 16), f32),
            jax.ShapeDtypeStruct((32, 1024), f32),
            jax.ShapeDtypeStruct((32, 512), f32),
        ),
        in_specs=[VM] * 7 + [ANY] * 4,
        out_specs=(VM,) * 5,
        scratch_shapes=[
            vm((2048, 512)), vm((2048, 1024)), vm((256, 2048)), vm((256, 2048)),
            vm((256, 512)), vm((256, 1024)),
            vm((256, 1024), f32), vm((256, 1024), f32),
            vm((256, 1024)), vm((256, 1024)), vm((256, 1024)), vm((256, 1024)),
            vm((256, 1024), f32), vm((256, 1024), f32), vm((256, 1024), f32),
            vm((2, 256, 256), f32), vm((256, 16), f32), vm((16, 256), f32),
            vm((16, 80, 128)), vm((16, 80, 128)), vm((16, 64, 128)), vm((16, 64, 128)),
            vm((16, 64, 128)), vm((16, 64, 128)), vm((16, 64, 128)), vm((16, 64, 128)),
            vm((3, 4, 256, 512)), vm((2, 4, 256, 512)),
            vm((256, 2048), f32), vm((128, 2048)), vm((128, 2048)), vm((128, 2048)), vm((128, 2048)),
            vm((3, 16, 32, 512), f32), vm((3, 7, 2, 32, 512)), vm((3, 7, 2, 32, 512)),
            vm((3, 32, 512)), vm((3, 32, 512)),
            dma((3, 12)), dma((3, 12)), dma((2, 4)), dma((2, 4)), dma((2, 4)), dma((2, 4)),
            dma((4, 16)), dma((4, 16)),
            dma((3, 6)), dma((3, 6)), dma((3, 7)), dma((3, 7)), dma((3,)), dma((3,)), dma((3,)), dma((3,)),
            dma((4,)),
        ],
        compiler_params=pltpu.CompilerParams(
            collective_id=1, has_side_effects=True, vmem_limit_bytes=LIMIT
        ),
        name="whole",
    )(x, raw, bias, rate, skip, start, stop, wi, wo, lin, up)


def per_device(
    layer_in, head_in, step_raw, step_bias, rate_log, skip_gain,
    inject_weight, out_weight, upstream, window_start, lengths,
):
    lg, hg, sg, wg, ig = call(
        head_in[0],
        step_raw[0],
        step_bias[None],
        rate_log[None],
        skip_gain[None],
        window_start[None],
        lengths[None],
        inject_weight.reshape(512, 512),
        out_weight,
        layer_in[0],
        upstream[0],
    )
    return lg[None], hg[None], sg[None], wg, ig.reshape(32, 2, 256)


def solution(mesh):
    placed = (
        P("dp", "ctx", None),
        P("dp", "ctx", "tensor"),
        P("dp", "ctx", "tensor"),
        P("tensor"),
        P("tensor"),
        P("tensor"),
        P("dp", "tensor", None),
        P("dp", "tensor"),
        P("dp", "ctx", None),
        P("dp"),
        P("dp"),
    )
    return jax.shard_map(
        per_device,
        mesh=mesh,
        in_specs=placed,
        out_specs=(
            P("dp", "ctx", None),
            P("dp", "ctx", "tensor"),
            P("dp", "ctx", "tensor"),
            P(("dp", "ctx"), "tensor"),
            P(("dp", "ctx"), "tensor", None),
        ),
        check_vma=False,
    )
```

time: 1310 us -> 129 us (0.10)
  waiting for transfers between devices: 1040 us -> 0 us
  Pallas kernels: 0 us -> 118 us
  blocking collectives: 85.4 us -> 0 us
  local copies, waits for them, and re-layouts: 67.4 us -> 9.01 us
  other arithmetic: 50.5 us -> 0 us
  matrix products: 48.5 us -> 0 us
  between operations: 16.7 us -> 1.97 us
    unnamed x8 -> x0, waiting for transfers between devices: 855 us -> none
    all_gather x4 -> x0, waiting for transfers between devices: 185 us -> none  [the longest x2 107 us: entering_2(): everything = jax.tree.map(lambda part: lax.all_gather(part, axis), x)]
    pallas_call x0 -> x1, Pallas kernels: none -> 118 us  [call(): pl.pallas_call(kernel, out_shape=(jax.ShapeDtypeStruct((256, 2048), bf16)...]
    psum x1 -> x0, blocking collectives: 49.7 us -> none  [per_device(): layer_grad = lax.psum(partial_value, 'tensor').astype(jnp.bfloat16)]
    dot_general x19 -> x0, matrix products: 48.5 us -> none  [the longest x3 12.5 us: block_parts(): jnp.einsum('ctsgj,csgjp->ctgjp', weighted, head_values, precision=highest)]
    select_n x32 -> x0, other arithmetic: 37.6 us -> none  [hop(): return jax.tree.map(lambda a, b: jnp.where(reached, a, b), new, before)]
    all_gather x1 -> x0, blocking collectives: 35.7 us -> none  [entering_2(): everything = jax.tree.map(lambda part: lax.all_gather(part, axis), x)]
    exp x33 -> x0, local copies, waits for them, and re-layouts: 21.3 us -> none  [the longest x32 21.3 us: chain_step(): jnp.exp(later[0])[..., None, None] * earlier[1] + later[1]]
  transfers between devices with their start and end apart: 6 -> 0, of which waited for: 6 -> 0; matrix products, arithmetic and copies ran while one was open for 9% -> 0% of each run, Pallas kernels for 0% -> 0%
where the time goes in v2:
time: 129 us
  Pallas kernels  118 us (91%)
  local copies, waits for them, and re-layouts  9.01 us (7%)
  between operations  1.97 us (2%)
    pallas_call x1, Pallas kernels, call(): pl.pallas_call(kernel, out_shape=(jax.ShapeDtypeStruct((256, 2048), bf16)...  118 us
    unnamed x14, local copies, waits for them, and re-layouts  8.34 us

profile of v2, /device:TPU:16, one launch (start us, length us, event | category | flops | bytes accessed | tf_op | source)
XLA Modules:
  0.0 129.0 jit_solution(12846269073461542558)
XLA Ops:
  0.6 0.0 copy-start.3
  1.9 0.0 copy-done.3
  2.0 0.8 copy.16
  2.7 1.9 %copy.18 = bf16[64,8,2,256]{3,1,2,0:T(8,128)(2,1)} copy(bf16[64,8,2,256]{3,2,1,0:T(2,128)(2,1)} %bitcast.21) | data formatting | bytes 1048576
  4.6 118.1 %whole.1 = (bf16[256,2048]{1,0:T(8,128)(2,1)}, bf16[256,1024]{1,0:T(8,128)(2,1)}, f32[256,16]{1,0:T(8,128)}, f32[32,1024]{1,0:T(8,128)}, f32[32,512]{1,0:T(8,128)}) custom-call(bf16[256,1024]{1,0:T(8,128)(2,1)} %bitcast.23, f32[256,16]{1,0:T(8,128)} %bitcast.20, f32[1,16]{1,0:T(1,128)} %bitcast.25, f32[1,16]{1,0:T(1,128)} %bitcast.26, f32[1,16]{1,0:T(1,128)} %bitcast.27, ...), custom_call_target="tpu_custom_call" | custom-call | tf_op jit(solution)/shard_map/whole/pallas_call | solution.py:567
  122.7 0.0 copy-start.2
  122.7 1.6 %copy.17 = f32[1,256,16]{1,2,0:T(8,128)} copy(f32[1,256,16]{2,1,0:T(8,128)} %bitcast.24) | data formatting | bytes 32768
  124.3 0.0 copy-done.2
  124.3 0.7 reshape.17
  125.0 0.0 copy-start
  125.0 2.4 %copy.24 = bf16[1,256,2048]{2,1,0:T(8,128)(2,1)} copy(bf16[1,256,2048]{2,1,0:T(8,128)(2,1)} %bitcast.17) | data formatting | bytes 2097152
  127.4 0.0 copy-done
  127.4 0.0 copy-start.1
  127.4 0.8 copy.25
  128.2 0.2 copy-done.1
  128.4 0.7 copy.26
Async XLA Ops:
  0.6 1.3 %copy-start.3 = (f32[1,256,16]{1,2,0:T(8,128)S(1)}, f32[1,256,16]{1,2,0:T(8,128)}, u32[]{:S(2)}) copy-start(f32[1,256,16]{1,2,0:T(8,128)} %param.13) | copy-start | bytes 49156
  122.7 1.6 %copy-start.2 = (f32[32,512]{1,0:T(8,128)S(1)}, f32[32,512]{1,0:T(8,128)}, u32[]{:S(2)}) copy-start(f32[32,512]{1,0:T(8,128)} %get-tuple-element.14) | copy-start | bytes 196612
  125.0 2.4 %copy-start = (bf16[256,1024]{1,0:T(8,128)(2,1)S(1)}, bf16[256,1024]{1,0:T(8,128)(2,1)}, u32[]{:S(2)}) copy-start(bf16[256,1024]{1,0:T(8,128)(2,1)} %get-tuple-element.11) | copy-start | bytes 1572868
  127.4 1.0 copy-start.1

commit v3 on v2

--- a/solution.py
+++ b/solution.py
@@ -10,7 +10,7 @@
 MESH = pl.DeviceIdType.MESH
 ANY = pl.BlockSpec(memory_space=pl.ANY)
 VM = pl.BlockSpec(memory_space=pltpu.VMEM)
-WINDOW = 2
+WINDOW = 3
 LIMIT = 56 * 1024 * 1024
 ROWS = (((0,), (0,)), ((), ()))
 COLS = (((1,), (1,)), ((), ()))
@@ -96,8 +96,8 @@
 def kernel(
     x_ref, raw_ref, bias_ref, rate_ref, skip_ref, start_ref, stop_ref, wi, wo, lin, up,
     lg, hg_ref, sg_ref, wg, ig,
-    wi_v, wo_v, lin_v, up_v, proj_s, back_s, y_s, z_s, xs_s, xe_s, dy_s, de_s, erx_s, etx_s, dtx_s, ds_s,
-    r_s, rt_s, f_out, f_got, f_mid, f_fin, b_out, b_got, b_mid, b_fin,
+    wi_v, wo_v, lin_v, up_v, proj_s, y_s, z_s, xs_s, xe_s, dy_s, de_s, erx_s, etx_s, dtx_s, ds_s,
+    r_s, rt_s, grow_s, w_s, f_out, f_got, f_mid, f_fin, b_out, b_got, b_mid, b_fin,
     factor, act, part, half_out, half_in, pair_out, pair_in, acc, ring_out, ring_in, y_out, y_in,
     wsend, wrecv, asend, arecv, csend, crecv, esend, erecv,
     send, recv, zsend, zrecv, ysend, yrecv, tsend, trecv, local,
@@ -127,7 +127,9 @@
         + [{"ctx": lax.rem(c + k, 16)} for k in range(1, 16)]
     )
 
-    links = {k: Lane(WINDOW) for k in ("right", "left", "up", "down")}
+    links = {k: Lane(WINDOW) for k in ("right", "left", "up", "down", "across")}
+    halves = (h, yl, h)
+    relays = (("up", "down"), ("across", "across"), ("up", "down"))
 
     def strip(ref, g):
         return ref if g == 0 else ref.at[:, 512 * (g - 1) : 512 * g]
@@ -137,11 +139,11 @@
         return strip(wi_v if g == 0 else wo_v, g).at[rows]
 
     def first(g, q, event, way):
-        rows = pl.ds(pl.multiple_of(h * 256 + q * 128, 128), 128)
+        rows = pl.ds(pl.multiple_of(halves[g] * 256 + q * 128, 128), 128)
         links[way].push(
             remote(
                 strip(wi if g == 0 else wo, g).at[rows],
-                weight_rows(g, x, h, q),
+                weight_rows(g, x, halves[g], q),
                 wsend.at[g, event],
                 wrecv.at[g, event],
                 at[way],
@@ -153,10 +155,11 @@
         remote(dst, dst, wsend.at[g, event], wrecv.at[g, event], at["left"]).wait_recv()
 
     def forward(g, slab, q, event, way):
-        dst = weight_rows(g, slab, h, q)
+        dst = weight_rows(g, slab, halves[g], q)
         links[way].push(remote(dst, dst, wsend.at[g, event], wrecv.at[g, event], at[way]))
 
     def slot(g, n):
+        h, (first_way, second_way) = halves[g], relays[g]
         if n == 0:
             first(g, 0, 0, "right")
             first(g, 1, 2, "left")
@@ -168,23 +171,23 @@
             forward(g, lefts, 0, 4, "right")
             arrived(g, rights, h, 1, 2)
             forward(g, rights, 1, 5, "left")
-            forward(g, lefts, 0, 6, "up")
-            forward(g, rights, 1, 10, "down")
+            forward(g, lefts, 0, 6, first_way)
+            forward(g, rights, 1, 10, second_way)
         elif n == 3:
             arrived(g, lefts, h, 1, 1)
-            forward(g, lefts, 1, 9, "down")
+            forward(g, lefts, 1, 9, second_way)
             arrived(g, rights, h, 0, 3)
-            forward(g, rights, 0, 7, "up")
+            forward(g, rights, 0, 7, first_way)
         else:
             arrived(g, opposite, h, 0, 4)
-            forward(g, opposite, 0, 8, "up")
+            forward(g, opposite, 0, 8, first_way)
             arrived(g, opposite, h, 1, 5)
-            forward(g, opposite, 1, 11, "down")
+            forward(g, opposite, 1, 11, second_way)
 
     def gathered(g):
         for n, slab in enumerate((lefts, rights, opposite)):
-            arrived(g, slab, 1 - h, 0, 6 + n)
-            arrived(g, slab, 1 - h, 1, 9 + n)
+            arrived(g, slab, 1 - halves[g], 0, 6 + n)
+            arrived(g, slab, 1 - halves[g], 1, 9 + n)
 
     def swap(e, src, dst):
         def to_peer(k):
@@ -228,7 +231,7 @@
     position = c * 256 + iota((256, 1), 0)
     mask = jnp.where((position >= start_ref[...]) & (position < stop_ref[...]), 1.0, 0.0)
     rate = jnp.exp(rate_ref[...])
-    shifted = raw_ref[...] + bias_ref[...]
+    shifted = split_right(eye, raw_ref[...], 3, COLS) + bias_ref[...]
     small = jnp.exp(-jnp.abs(shifted))
     dt = mask * (jnp.maximum(shifted, 0.0) + jnp.log1p(small))
     sig = mask * jnp.where(shifted >= 0.0, 1.0, small) / (1.0 + small)
@@ -255,6 +258,8 @@
     slot(0, 3)
     slot(1, 1)
     slot(0, 4)
+    slot(1, 2)
+    slot(2, 0)
     for load in loads:
         load.wait()
     gathered(0)
@@ -273,12 +278,12 @@
         own = dot(xe_s[:, spans(g)], bs(g), ROWS)
         f_out[8 * g : 8 * g + 8, 0:64, :] = own.reshape(8, 64, 128).astype(bf16)
     f1[0]()
-    slot(1, 2)
-    slot(2, 0)
     slot(1, 3)
     slot(2, 1)
     slot(1, 4)
     slot(2, 2)
+    slot(2, 3)
+    slot(2, 4)
 
     def grow_of(k):
         lines = f_got[k, 64:80, :].astype(f32)
@@ -292,18 +297,22 @@
 
     lax.fori_loop(0, 16, ahead, jnp.zeros((64, 128), f32))
     f2[0]()
-    slot(2, 3)
-    slot(2, 4)
 
     values = (up_v, lin_v)
     acts = []
+
+    def token_rows(r):
+        return pl.ds(pl.multiple_of(r * 64, 64), 64)
+
+    far_t, core_t = lax.rem(t + 2, 4), t + 1 - 2 * cr
+    fourth_t = lax.rem(core_t + 2, 4)
 
     def act_send(n):
         for k in (1, 3, 2):
             to = lax.rem(x + k, 4)
             copy = remote(
-                values[n].at[mine, quarter(to)],
-                act.at[n, x, mine],
+                values[n].at[token_rows(t), quarter(to)],
+                act.at[n, x, token_rows(t)],
                 asend.at[n, k],
                 arecv.at[n, k],
                 {"dp": to},
@@ -312,67 +321,93 @@
             acts.append(copy)
         act[n, x] = values[n][:, quarter(x)]
 
+    def act_move(n, k, r, event, way):
+        dst = act.at[n, lax.rem(x + 4 - k, 4), token_rows(r)]
+        return remote(dst, dst, csend.at[n, k, event], crecv.at[n, k, event], at[way])
+
     def act_share(n):
         for k in (1, 3, 2):
-            dst = act.at[n, lax.rem(x + 4 - k, 4), mine]
+            dst = act.at[n, lax.rem(x + 4 - k, 4), token_rows(t)]
             remote(dst, dst, asend.at[n, k], arecv.at[n, k], at["left"]).wait_recv()
-            copy = remote(dst, dst, csend.at[n, k], crecv.at[n, k], at["core"])
+            for event, way in ((0, "far"), (1, "core")):
+                copy = act_move(n, k, t, event, way)
+                copy.start()
+                acts.append(copy)
+
+    def act_pass(n):
+        for k in (1, 3, 2):
+            act_move(n, k, far_t, 0, "far").wait_recv()
+            copy = act_move(n, k, far_t, 2, "core")
             copy.start()
             acts.append(copy)
 
     def act_done(n):
         for k in (1, 3, 2):
-            dst = act.at[n, lax.rem(x + 4 - k, 4), other]
-            remote(dst, dst, csend.at[n, k], crecv.at[n, k], at["core"]).wait_recv()
+            act_move(n, k, core_t, 1, "core").wait_recv()
+            act_move(n, k, fourth_t, 2, "core").wait_recv()
+
+    side = iota((256, 128), 1)
+    side16 = iota((256, 16), 1)
+    low_side = side < 64
+
+    def half_of(v, half):
+        return jnp.where(low_side if half == 0 else ~low_side, v, jnp.zeros_like(v))
+
+    def lanes_of(g, p):
+        return pl.ds(pl.multiple_of(512 * g + p * 128, 128), 128)
+
+    def ahead_group(g):
+        scores = dot(cs(g), bs(g), COLS)
+
+        def pair(p, carry):
+            x2 = xs_s[:, lanes_of(g, p)]
+            y2 = jnp.zeros((256, 128), f32)
+            for half in range(2):
+                head = 8 * g + 2 * p + half
+                col = jnp.sum(jnp.where(side16 == head, r_s[...], 0.0), axis=1, keepdims=True)
+                line = rt_s[pl.ds(head, 1), :]
+                grow = jnp.exp(jnp.where(above, col - line, -1e30))
+                w = (scores * grow).astype(bf16)
+                grow_s[head] = grow
+                w_s[head] = w
+                y2 += dot(w, half_of(x2, half))
+            y_s[:, lanes_of(g, p)] = y2
+            return carry
+
+        lax.fori_loop(0, 4, pair, 0)
+
+    def back_group(g):
+        ds_s[g] = jnp.zeros((256, 256), f32)
+
+        def pair(p, carry):
+            x2 = xs_s[:, lanes_of(g, p)]
+            dy2 = dy_s[:, lanes_of(g, p)]
+            z2 = jnp.zeros((256, 128), f32)
+            ds = ds_s[g]
+            for half in range(2):
+                head = 8 * g + 2 * p + half
+                dm = half_of(dy2, half)
+                z2 += dot(w_s[head], dm, ROWS)
+                ds += dot(dm, half_of(x2, half), COLS) * grow_s[head]
+            z_s[:, lanes_of(g, p)] = z2
+            ds_s[g] = ds
+            return carry
+
+        lax.fori_loop(0, 4, pair, 0)
 
     act_send(0)
+    act_send(1)
+    ahead_group(0)
+    ahead_group(1)
     gathered(1)
+    dy_s[:, 0:512] = (dot(up_v[...], wo_v[:, 0:512]).astype(bf16).astype(f32) * mask).astype(bf16)
     gathered(2)
-    act_send(1)
-    back = dot(up_v[...], wo_v[...]).astype(bf16).astype(f32)
-    dy_s[...] = (back * mask).astype(bf16)
+    dy_s[:, 512:] = (dot(up_v[...], wo_v[:, 512:]).astype(bf16).astype(f32) * mask).astype(bf16)
     de_s[...] = (dy_s[...].astype(f32) * erx_s[...]).astype(bf16)
     for g in range(2):
         pull = dot(de_s[:, spans(g)], cs(g), ROWS)
         b_out[8 * g : 8 * g + 8] = pull.reshape(8, 64, 128).astype(bf16)
     b1[0]()
-
-    side = iota((256, 128), 1)
-    side16 = iota((256, 16), 1)
-
-    def group(g):
-        bg, cg = bs(g), cs(g)
-        scores = dot(cg, bg, COLS)
-        ds_s[g] = jnp.zeros((256, 256), f32)
-
-        def pair(p, carry):
-            lanes = pl.ds(pl.multiple_of(512 * g + p * 128, 128), 128)
-            x2 = xs_s[:, lanes]
-            dy2 = dy_s[:, lanes]
-            y2 = jnp.zeros((256, 128), f32)
-            z2 = jnp.zeros((256, 128), f32)
-            ds = ds_s[g]
-            for half in range(2):
-                head = 8 * g + 2 * p + half
-                col = jnp.sum(jnp.where(side16 == head, r_s[...], 0.0), axis=1, keepdims=True)
-                line = rt_s[pl.ds(head, 1), :]
-                grow = jnp.exp(jnp.where(above, col - line, -1e30))
-                here = (side >= 64) if half else (side < 64)
-                xm = jnp.where(here, x2, jnp.zeros_like(x2))
-                dm = jnp.where(here, dy2, jnp.zeros_like(dy2))
-                w = (scores * grow).astype(bf16)
-                y2 += dot(w, xm)
-                z2 += dot(w, dm, ROWS)
-                ds += dot(dm, xm, COLS) * grow
-            y_s[:, lanes] = y2
-            z_s[:, lanes] = z2
-            ds_s[g] = ds
-            return carry
-
-        lax.fori_loop(0, 4, pair, 0)
-
-    group(0)
-    group(1)
 
     def states(fin, g):
         return fin[8 * g : 8 * g + 8].reshape(512, 128)
@@ -409,6 +444,10 @@
         value = mask * (yt + skipx[:, span] * x_ref[:, span].astype(f32))
         factor[g, x] = value.astype(bf16)
         own_send(g)
+    act_share(0)
+    act_share(1)
+    back_group(0)
+    back_group(1)
 
     b1[1]()
 
@@ -419,10 +458,10 @@
 
     lax.fori_loop(0, 16, behind, jnp.zeros((64, 128), f32))
     b2[0]()
-    act_share(0)
+    act_pass(0)
+    act_pass(1)
     relay(0)
     relay(1)
-    act_share(1)
     b2[1]()
 
     for g in range(2):
@@ -488,7 +527,8 @@
         if g < 2:
             wg[:, 512 * g : 512 * g + 512] = total
         else:
-            ig[...] = total
+            ig[:, 0, :] = total[:, 0:256]
+            ig[:, 1, :] = total[:, 256:512]
 
     act_done(0)
     product(0)
@@ -571,24 +611,23 @@
             jax.ShapeDtypeStruct((256, 1024), bf16),
             jax.ShapeDtypeStruct((256, 16), f32),
             jax.ShapeDtypeStruct((32, 1024), f32),
-            jax.ShapeDtypeStruct((32, 512), f32),
+            jax.ShapeDtypeStruct((32, 2, 256), f32),
         ),
         in_specs=[VM] * 7 + [ANY] * 4,
         out_specs=(VM,) * 5,
         scratch_shapes=[
             vm((2048, 512)), vm((2048, 1024)), vm((256, 2048)), vm((256, 2048)),
-            vm((256, 512)), vm((256, 1024)),
-            vm((256, 1024), f32), vm((256, 1024), f32),
+            vm((256, 512)), vm((256, 1024), f32), vm((256, 1024), f32),
             vm((256, 1024)), vm((256, 1024)), vm((256, 1024)), vm((256, 1024)),
             vm((256, 1024), f32), vm((256, 1024), f32), vm((256, 1024), f32),
-            vm((2, 256, 256), f32), vm((256, 16), f32), vm((16, 256), f32),
+            vm((2, 256, 256), f32), vm((256, 16), f32), vm((16, 256), f32), vm((16, 256, 256), f32), vm((16, 256, 256)),
             vm((16, 80, 128)), vm((16, 80, 128)), vm((16, 64, 128)), vm((16, 64, 128)),
             vm((16, 64, 128)), vm((16, 64, 128)), vm((16, 64, 128)), vm((16, 64, 128)),
             vm((3, 4, 256, 512)), vm((2, 4, 256, 512)),
             vm((256, 2048), f32), vm((128, 2048)), vm((128, 2048)), vm((128, 2048)), vm((128, 2048)),
             vm((3, 16, 32, 512), f32), vm((3, 7, 2, 32, 512)), vm((3, 7, 2, 32, 512)),
             vm((3, 32, 512)), vm((3, 32, 512)),
-            dma((3, 12)), dma((3, 12)), dma((2, 4)), dma((2, 4)), dma((2, 4)), dma((2, 4)),
+            dma((3, 12)), dma((3, 12)), dma((2, 4)), dma((2, 4)), dma((2, 4, 3)), dma((2, 4, 3)),
             dma((4, 16)), dma((4, 16)),
             dma((3, 6)), dma((3, 6)), dma((3, 7)), dma((3, 7)), dma((3,)), dma((3,)), dma((3,)), dma((3,)),
             dma((4,)),
@@ -606,7 +645,7 @@
 ):
     lg, hg, sg, wg, ig = call(
         head_in[0],
-        step_raw[0],
+        step_raw[0].T,
         step_bias[None],
         rate_log[None],
         skip_gain[None],
@@ -617,7 +656,7 @@
         layer_in[0],
         upstream[0],
     )
-    return lg[None], hg[None], sg[None], wg, ig.reshape(32, 2, 256)
+    return lg[None], hg[None], sg[None], wg, ig
 
 
 def solution(mesh):

time: 129 us -> 119 us (0.922)
  Pallas kernels: 118 us -> 108 us
    pallas_call x1, Pallas kernels: 118 us -> 108 us  [call(): pl.pallas_call(kernel, out_shape=(jax.ShapeDtypeStruct((256, 2048), bf16)...]
    unnamed x14 -> x12, local copies, waits for them, and re-layouts: 8.34 us -> 8.38 us
where the time goes in v3:
time: 119 us
  Pallas kernels  108 us (91%)
  local copies, waits for them, and re-layouts  8.38 us (7%)
  between operations  1.94 us (2%)
    pallas_call x1, Pallas kernels, call(): pl.pallas_call(kernel, out_shape=(jax.ShapeDtypeStruct((256, 2048), bf16)...  108 us
    unnamed x12, local copies, waits for them, and re-layouts  8.38 us

profile of v3, /device:TPU:16, one launch (start us, length us, event | category | flops | bytes accessed | tf_op | source)
XLA Modules:
  0.0 118.6 jit_solution(5774745431763325375)
XLA Ops:
  1.9 1.9 %copy.17 = bf16[64,8,2,256]{3,1,2,0:T(8,128)(2,1)} copy(bf16[64,8,2,256]{3,2,1,0:T(2,128)(2,1)} %bitcast.22) | data formatting | bytes 1048576
  3.8 108.3 %whole.1 = (bf16[256,2048]{1,0:T(8,128)(2,1)}, bf16[256,1024]{1,0:T(8,128)(2,1)}, f32[256,16]{1,0:T(8,128)}, f32[32,1024]{1,0:T(8,128)}, f32[32,2,256]{2,1,0:T(2,128)}) custom-call(bf16[256,1024]{1,0:T(8,128)(2,1)} %bitcast.24, f32[16,256]{1,0:T(8,128)} %bitcast.26, f32[1,16]{1,0:T(1,128)} %bitcast.27, f32[1,16]{1,0:T(1,128)} %bitcast.28, f32[1,16]{1,0:T(1,128)} %bitcast.29, ...), custom_call_target="tpu_custom_call" | custom-call | tf_op jit(solution)/shard_map/whole/pallas_call | solution.py:607
  112.1 1.6 %copy.16 = f32[1,256,16]{1,2,0:T(8,128)} copy(f32[1,256,16]{2,1,0:T(8,128)} %bitcast.25) | data formatting | bytes 32768
  113.7 0.0 copy-start
  113.7 2.4 %copy.24 = bf16[1,256,2048]{2,1,0:T(8,128)(2,1)} copy(bf16[1,256,2048]{2,1,0:T(8,128)(2,1)} %bitcast.19) | data formatting | bytes 2097152
  116.1 0.0 copy-done
  116.1 0.0 copy-start.1
  116.1 0.8 copy.25
  116.9 0.2 copy-done.1
  117.1 0.0 copy-start.2
  117.1 0.7 copy.26
  117.8 0.2 copy-done.2
  118.0 0.6 copy.27
Async XLA Ops:
  113.7 2.4 %copy-start = (bf16[256,1024]{1,0:T(8,128)(2,1)S(1)}, bf16[256,1024]{1,0:T(8,128)(2,1)}, u32[]{:S(2)}) copy-start(bf16[256,1024]{1,0:T(8,128)(2,1)} %get-tuple-element.11) | copy-start | bytes 1572868
  116.1 1.0 copy-start.1
  117.1 0.9 copy-start.2

commit v4 on v3

--- a/solution.py
+++ b/solution.py
@@ -418,14 +418,25 @@
         copy.start()
         sent.append(copy)
 
+    def view(ref, g, *index):
+        if g < 2:
+            return ref.at[(g,) + index]
+        tail = (slice(None),) * (len(ref.shape) - 2 - len(index))
+        return ref.at[(2,) + index + tail + (slice(256 * g - 512, 256 * g - 256),)]
+
+    def rows_of(g, slab, q):
+        rows = pl.ds(128 * q, 128)
+        if g < 2:
+            return factor.at[g, slab, rows]
+        return factor.at[2, slab, rows, 256 * g - 512 : 256 * g - 256]
+
     def own_send(g):
-        rows = [pl.ds(0, 128), pl.ds(128, 128)]
         for q, event, way in ((0, 0, "right"), (1, 2, "left"), (1, 1, "right"), (0, 3, "left")):
-            src = factor.at[g, x, rows[q]]
+            src = rows_of(g, x, q)
             go(remote(src, src, send.at[g, event], recv.at[g, event], at[way]))
 
     def came(g, slab, q, event):
-        dst = factor.at[g, slab, pl.ds(128 * q, 128)]
+        dst = rows_of(g, slab, q)
         remote(dst, dst, send.at[g, event], recv.at[g, event], at["left"]).wait_recv()
         return dst
 
@@ -472,7 +483,7 @@
         dc = dot(dsr, bs(g)) + dot(de_s[:, spans(g)], state)
         factor[2, x, :, 256 * g : 256 * g + 128] = db.astype(bf16)
         factor[2, x, :, 256 * g + 128 : 256 * g + 256] = dc.astype(bf16)
-    own_send(2)
+        own_send(2 + g)
     part[...] = dot(factor[2, x], wi_v[...], COLS)
     half_out[...] = part[other, :].astype(bf16)
     go(remote(half_out, half_in, tsend.at[0], trecv.at[0], at["core"]))
@@ -483,26 +494,28 @@
         came(g, opposite, 0, 4)
         came(g, opposite, 1, 5)
         a = act[0 if g < 2 else 1].reshape(1024, 512)
-        acc[g] = dot(a, factor[g].reshape(1024, 512), ROWS).reshape(16, 32, 512)
+        if g < 2:
+            acc[g] = dot(a, factor[g].reshape(1024, 512), ROWS).reshape(16, 32, 512)
+        else:
+            lanes = slice(256 * g - 512, 256 * g - 256)
+            right = factor[2, :, :, lanes].reshape(1024, 256)
+            acc[2, :, :, lanes] = dot(a, right, ROWS).reshape(16, 32, 256)
+
+    def arrival(g, n):
+        got = view(ring_in, g, n)
+        remote(got, got, zsend.at[g, n], zrecv.at[g, n], at["up"]).wait_recv()
+        return got[0].astype(f32), got[1].astype(f32)
 
     def pass_on(g, k, slot_in, slot_out, way):
-        low, high = acc[g, k], acc[g, 8 + k]
+        low, high = view(acc, g, k)[...], view(acc, g, 8 + k)[...]
         if slot_in is not None:
-            got = ring_in.at[g, slot_in]
-            remote(got, got, zsend.at[g, slot_in], zrecv.at[g, slot_in], at["up"]).wait_recv()
-            low += got[0].astype(f32)
-            high += got[1].astype(f32)
-        ring_out[g, slot_out, 0] = low.astype(bf16)
-        ring_out[g, slot_out, 1] = high.astype(bf16)
-        go(
-            remote(
-                ring_out.at[g, slot_out],
-                ring_in.at[g, slot_out],
-                zsend.at[g, slot_out],
-                zrecv.at[g, slot_out],
-                at[way],
-            )
-        )
+            more = arrival(g, slot_in)
+            low += more[0]
+            high += more[1]
+        src, dst = view(ring_out, g, slot_out), view(ring_in, g, slot_out)
+        src[0] = low.astype(bf16)
+        src[1] = high.astype(bf16)
+        go(remote(src, dst, zsend.at[g, slot_out], zrecv.at[g, slot_out], at[way]))
 
     def ring(g, s):
         if s < 4:
@@ -510,46 +523,34 @@
         if s < 3:
             pass_on(g, lax.rem(z + 5 + s, 8), s + 3 if s else None, s + 4, "down")
         if s == 4:
-            low, high = acc[g, z], acc[g, 8 + z]
+            low, high = view(acc, g, z)[...], view(acc, g, 8 + z)[...]
             for n in (3, 6):
-                got = ring_in.at[g, n]
-                remote(got, got, zsend.at[g, n], zrecv.at[g, n], at["up"]).wait_recv()
-                low += got[0].astype(f32)
-                high += got[1].astype(f32)
-            acc[g, z] = low
-            acc[g, 8 + z] = high
-            y_out[g] = acc[g, (1 - yl) * 8 + z].astype(bf16)
-            go(remote(y_out.at[g], y_in.at[g], ysend.at[g], yrecv.at[g], at["across"]))
+                more = arrival(g, n)
+                low += more[0]
+                high += more[1]
+            view(acc, g, z)[...] = low
+            view(acc, g, 8 + z)[...] = high
+            src, dst = view(y_out, g), view(y_in, g)
+            src[...] = view(acc, g, (1 - yl) * 8 + z)[...].astype(bf16)
+            go(remote(src, dst, ysend.at[g], yrecv.at[g], at["across"]))
 
     def finish(g):
-        remote(y_out.at[g], y_in.at[g], ysend.at[g], yrecv.at[g], at["across"]).wait_recv()
-        total = acc[g, c] + y_in[g].astype(f32)
+        src, dst = view(y_out, g), view(y_in, g)
+        remote(src, dst, ysend.at[g], yrecv.at[g], at["across"]).wait_recv()
+        total = view(acc, g, c)[...] + dst[...].astype(f32)
         if g < 2:
             wg[:, 512 * g : 512 * g + 512] = total
         else:
-            ig[:, 0, :] = total[:, 0:256]
-            ig[:, 1, :] = total[:, 256:512]
-
-    act_done(0)
-    product(0)
-    ring(0, 0)
-    relay(2)
-    product(1)
-    ring(1, 0)
-    ring(0, 1)
-    ring(1, 1)
-    remote(half_out, half_in, tsend.at[0], trecv.at[0], at["core"]).wait_recv()
-    pair_out[...] = (part[mine, :] + half_in[...].astype(f32)).astype(bf16)
-    go(remote(pair_out, pair_in, tsend.at[1], trecv.at[1], at["far"]))
-    ring(0, 2)
-    ring(1, 2)
+            ig[:, 256 * g - 512 : 256 * g - 256] = total
 
     sums_q = jnp.zeros((256, 16), f32)
     sums_v = jnp.zeros((256, 16), f32)
     sums_u = jnp.zeros((256, 16), f32)
     ends = jnp.zeros((8, 16), f32)
+    sums = (sums_q, sums_v, sums_u, ends)
     ones = jnp.ones((8, 128), bf16)
-    for g in range(2):
+    def rest(g, sums):
+        sums_q, sums_v, sums_u, ends = sums
         span = spans(g)
         later, state = states(b_fin, g), states(f_fin, g)
         ex = expand[:, span]
@@ -565,28 +566,53 @@
         sums_u += split_left(xg * zt, ex, 2, COLS)
         rows = split_right(ones, state.astype(f32) * later.astype(f32), 2, COLS)
         ends += split_left(rows, ex, 2, COLS)
+        return sums_q, sums_v, sums_u, ends
+
+    act_done(0)
+    product(0)
+    ring(0, 0)
+    relay(2)
+    product(1)
+    ring(1, 0)
+    ring(0, 1)
+    relay(3)
+    ring(1, 1)
+    remote(half_out, half_in, tsend.at[0], trecv.at[0], at["core"]).wait_recv()
+    pair_out[...] = (part[mine, :] + half_in[...].astype(f32)).astype(bf16)
+    go(remote(pair_out, pair_in, tsend.at[1], trecv.at[1], at["far"]))
+    act_done(1)
+    product(2)
+    ring(2, 0)
+    ring(0, 2)
+    ring(1, 2)
+    sums = rest(0, sums)
+    product(3)
+    ring(3, 0)
+    ring(2, 1)
+    ring(0, 3)
+    ring(1, 3)
+    ring(3, 1)
+    ring(2, 2)
+    sums = rest(1, sums)
+    ring(3, 2)
+    ring(2, 3)
+    ring(0, 4)
+    ring(1, 4)
+    ring(3, 3)
+    remote(pair_out, pair_in, tsend.at[1], trecv.at[1], at["far"]).wait_recv()
+    lg[mine, :] = (pair_out[...].astype(f32) + pair_in[...].astype(f32)).astype(bf16)
+    go(remote(lg.at[mine], lg.at[mine], tsend.at[2], trecv.at[2], at["core"]))
+    ring(2, 4)
+    ring(3, 4)
+    sums_q, sums_v, sums_u, ends = sums
     triu = jnp.where(iota((256, 256), 0) <= iota((256, 256), 1), 1.0, 0.0).astype(bf16)
     lower = jnp.where(iota((256, 256), 0) > iota((256, 256), 1), 1.0, 0.0).astype(bf16)
     flow = split_right(triu, sums_q, 3) + split_right(lower, sums_v, 3)
     flow = flow + ends[0:1, :] * jnp.exp(last)
     sg_ref[...] = sig * (sums_u - rate * flow)
 
-    act_done(1)
-    product(2)
-    ring(2, 0)
-    ring(0, 3)
-    ring(1, 3)
-    ring(2, 1)
-    remote(pair_out, pair_in, tsend.at[1], trecv.at[1], at["far"]).wait_recv()
-    lg[mine, :] = (pair_out[...].astype(f32) + pair_in[...].astype(f32)).astype(bf16)
-    go(remote(lg.at[mine], lg.at[mine], tsend.at[2], trecv.at[2], at["core"]))
-    ring(2, 2)
-    ring(0, 4)
-    ring(1, 4)
-    ring(2, 3)
     finish(0)
     finish(1)
-    ring(2, 4)
     for lane in links.values():
         lane.drain()
     for copy in acts:
@@ -594,12 +620,13 @@
     for e in (f1, f2, b1, b2):
         e[2]()
     finish(2)
+    finish(3)
     remote(lg.at[other], lg.at[other], tsend.at[2], trecv.at[2], at["core"]).wait_recv()
     for copy in sent:
         copy.wait_send()
 
 
-def call(x, raw, bias, rate, skip, start, stop, wi, wo, lin, up):
+def whole(x, raw, bias, rate, skip, start, stop, wi, wo, lin, up):
     def vm(shape, kind=bf16):
         return pltpu.VMEM(shape, kind)
 
@@ -611,7 +638,7 @@
             jax.ShapeDtypeStruct((256, 1024), bf16),
             jax.ShapeDtypeStruct((256, 16), f32),
             jax.ShapeDtypeStruct((32, 1024), f32),
-            jax.ShapeDtypeStruct((32, 2, 256), f32),
+            jax.ShapeDtypeStruct((32, 512), f32),
         ),
         in_specs=[VM] * 7 + [ANY] * 4,
         out_specs=(VM,) * 5,
@@ -629,7 +656,7 @@
             vm((3, 32, 512)), vm((3, 32, 512)),
             dma((3, 12)), dma((3, 12)), dma((2, 4)), dma((2, 4)), dma((2, 4, 3)), dma((2, 4, 3)),
             dma((4, 16)), dma((4, 16)),
-            dma((3, 6)), dma((3, 6)), dma((3, 7)), dma((3, 7)), dma((3,)), dma((3,)), dma((3,)), dma((3,)),
+            dma((4, 6)), dma((4, 6)), dma((4, 7)), dma((4, 7)), dma((4,)), dma((4,)), dma((3,)), dma((3,)),
             dma((4,)),
         ],
         compiler_params=pltpu.CompilerParams(
@@ -637,6 +664,30 @@
         ),
         name="whole",
     )(x, raw, bias, rate, skip, start, stop, wi, wo, lin, up)
+
+
+def settle_kernel(lg, hg, sg, wg, ig, lg_out, hg_out, sg_out, wg_out, ig_out):
+    lg_out[...] = lg[...]
+    hg_out[...] = hg[...]
+    sg_out[...] = sg[...]
+    wg_out[...] = wg[...]
+    ig_out[:, 0, :] = ig[:, 0:256]
+    ig_out[:, 1, :] = ig[:, 256:512]
+
+
+def settle(*found):
+    shapes = [(v.shape, v.dtype) for v in found[:4]] + [((32, 2, 256), f32)]
+    return pl.pallas_call(
+        settle_kernel,
+        out_shape=tuple(jax.ShapeDtypeStruct(*kind) for kind in shapes),
+        in_specs=[VM] * 5,
+        out_specs=(VM,) * 5,
+        name="settle",
+    )(*found)
+
+
+def call(*inputs):
+    return settle(*whole(*inputs))
 
 
 def per_device(

time: 119 us -> 113 us (0.950)
  local copies, waits for them, and re-layouts: 8.38 us -> 3.5 us
    unnamed x12 -> x2, local copies, waits for them, and re-layouts: 8.38 us -> 3.5 us
    pallas_call x1 -> x2, Pallas kernels: 108 us -> 108 us  [the longest x1 105 us: whole(): pl.pallas_call(kernel, out_shape=(jax.ShapeDtypeStruct((256, 2048), bf16)...]
where the time goes in v4:
time: 113 us
  Pallas kernels  108 us (96%)
  local copies, waits for them, and re-layouts  3.5 us (3%)
  between operations  1.93 us (2%)
    pallas_call x1, Pallas kernels, whole(): pl.pallas_call(kernel, out_shape=(jax.ShapeDtypeStruct((256, 2048), bf16)...  105 us
    unnamed x2, local copies, waits for them, and re-layouts  3.5 us
    pallas_call x1, Pallas kernels, settle(): pl.pallas_call(settle_kernel, out_shape=tuple((jax.ShapeDtypeStruct(*kind...  2.7 us

profile of v4, /device:TPU:16, one launch (start us, length us, event | category | flops | bytes accessed | tf_op | source)
XLA Modules:
  0.0 113.3 jit_solution(10055510685878057522)
XLA Ops:
  1.9 1.9 %copy.17 = bf16[64,8,2,256]{3,1,2,0:T(8,128)(2,1)} copy(bf16[64,8,2,256]{3,2,1,0:T(2,128)(2,1)} %bitcast.21) | data formatting | bytes 1048576
  3.8 105.1 %whole.1 = (bf16[256,2048]{1,0:T(8,128)(2,1)}, bf16[256,1024]{1,0:T(8,128)(2,1)}, f32[256,16]{1,0:T(8,128)}, f32[32,1024]{1,0:T(8,128)}, f32[32,512]{1,0:T(8,128)}) custom-call(bf16[256,1024]{1,0:T(8,128)(2,1)} %bitcast.22, f32[16,256]{1,0:T(8,128)} %bitcast.24, f32[1,16]{1,0:T(1,128)} %bitcast.25, f32[1,16]{1,0:T(1,128)} %bitcast.26, f32[1,16]{1,0:T(1,128)} %bitcast.27, ...), custom_call_target="tpu_custom_call" | custom-call | tf_op jit(solution)/shard_map/whole/pallas_call | solution.py:634
  109.0 2.7 %settle.1 = (bf16[256,2048]{1,0:T(8,128)(2,1)}, bf16[256,1024]{1,0:T(8,128)(2,1)}, f32[256,16]{1,0:T(8,128)}, f32[32,1024]{1,0:T(8,128)}, f32[32,2,256]{2,1,0:T(2,128)}) custom-call(bf16[256,2048]{1,0:T(8,128)(2,1)} %get-tuple-element.15.lg, bf16[256,1024]{1,0:T(8,128)(2,1)} %get-tuple-element.16.hg, f32[256,16]{1,0:T(8,128)} %get-tuple-element.17.sg, ...), custom_call_target="tpu_custom_call" | custom-call | tf_op jit(solution)/shard_map/settle/pallas_call | solution.py:680
  111.7 1.6 %copy.16 = f32[1,256,16]{1,2,0:T(8,128)} copy(f32[1,256,16]{2,1,0:T(8,128)} %bitcast.23) | data formatting | bytes 32768

commit v5 on v4

--- a/solution.py
+++ b/solution.py
@@ -98,7 +98,7 @@
     lg, hg_ref, sg_ref, wg, ig,
     wi_v, wo_v, lin_v, up_v, proj_s, y_s, z_s, xs_s, xe_s, dy_s, de_s, erx_s, etx_s, dtx_s, ds_s,
     r_s, rt_s, grow_s, w_s, f_out, f_got, f_mid, f_fin, b_out, b_got, b_mid, b_fin,
-    factor, act, part, half_out, half_in, pair_out, pair_in, acc, ring_out, ring_in, y_out, y_in,
+    factor, act, part, half_out, half_in, pair_out, pair_in, acc, ring_out, ring_in, y_out, y_in, d_out, d_got,
     wsend, wrecv, asend, arecv, csend, crecv, esend, erecv,
     send, recv, zsend, zrecv, ysend, yrecv, tsend, trecv, local,
 ):
@@ -203,7 +203,7 @@
                 fn(k)
                 return carry
 
-            lax.fori_loop(1, 16, step, 0)
+            lax.fori_loop(1, 16, step, 0, unroll=True)
 
         def begin():
             each(lambda k: to_peer(k).start())
@@ -219,6 +219,7 @@
     f2 = swap(1, f_mid, f_fin)
     b1 = swap(2, b_out, b_got)
     b2 = swap(3, b_mid, b_fin)
+    sums_out = {2: swap(4, d_out.at[0], d_got.at[0]), 3: swap(5, d_out.at[1], d_got.at[1])}
 
     slot(0, 0)
     slot(0, 1)
@@ -283,7 +284,6 @@
     slot(1, 4)
     slot(2, 2)
     slot(2, 3)
-    slot(2, 4)
 
     def grow_of(k):
         lines = f_got[k, 64:80, :].astype(f32)
@@ -295,8 +295,9 @@
         f_mid[k] = state.astype(bf16)
         return grow_of(k) * state + f_got[k, 0:64, :].astype(f32)
 
-    lax.fori_loop(0, 16, ahead, jnp.zeros((64, 128), f32))
+    lax.fori_loop(0, 16, ahead, jnp.zeros((64, 128), f32), unroll=True)
     f2[0]()
+    slot(2, 4)
 
     values = (up_v, lin_v)
     acts = []
@@ -401,14 +402,6 @@
     ahead_group(1)
     gathered(1)
     dy_s[:, 0:512] = (dot(up_v[...], wo_v[:, 0:512]).astype(bf16).astype(f32) * mask).astype(bf16)
-    gathered(2)
-    dy_s[:, 512:] = (dot(up_v[...], wo_v[:, 512:]).astype(bf16).astype(f32) * mask).astype(bf16)
-    de_s[...] = (dy_s[...].astype(f32) * erx_s[...]).astype(bf16)
-    for g in range(2):
-        pull = dot(de_s[:, spans(g)], cs(g), ROWS)
-        b_out[8 * g : 8 * g + 8] = pull.reshape(8, 64, 128).astype(bf16)
-    b1[0]()
-
     def states(fin, g):
         return fin[8 * g : 8 * g + 8].reshape(512, 128)
 
@@ -455,6 +448,14 @@
         value = mask * (yt + skipx[:, span] * x_ref[:, span].astype(f32))
         factor[g, x] = value.astype(bf16)
         own_send(g)
+    gathered(2)
+    dy_s[:, 512:] = (dot(up_v[...], wo_v[:, 512:]).astype(bf16).astype(f32) * mask).astype(bf16)
+    de_s[...] = (dy_s[...].astype(f32) * erx_s[...]).astype(bf16)
+    for g in range(2):
+        pull = dot(de_s[:, spans(g)], cs(g), ROWS)
+        b_out[8 * g : 8 * g + 8] = pull.reshape(8, 64, 128).astype(bf16)
+    b1[0]()
+
     act_share(0)
     act_share(1)
     back_group(0)
@@ -467,7 +468,7 @@
         b_mid[k] = state.astype(bf16)
         return grow_of(k) * state + b_got[k].astype(f32)
 
-    lax.fori_loop(0, 16, behind, jnp.zeros((64, 128), f32))
+    lax.fori_loop(0, 16, behind, jnp.zeros((64, 128), f32), unroll=True)
     b2[0]()
     act_pass(0)
     act_pass(1)
@@ -582,28 +583,22 @@
     go(remote(pair_out, pair_in, tsend.at[1], trecv.at[1], at["far"]))
     act_done(1)
     product(2)
-    ring(2, 0)
+    d_out[0] = view(acc, 2)[...].astype(bf16)
+    sums_out[2][0]()
     ring(0, 2)
     ring(1, 2)
     sums = rest(0, sums)
     product(3)
-    ring(3, 0)
-    ring(2, 1)
+    d_out[1] = view(acc, 3)[...].astype(bf16)
+    sums_out[3][0]()
     ring(0, 3)
     ring(1, 3)
-    ring(3, 1)
-    ring(2, 2)
     sums = rest(1, sums)
-    ring(3, 2)
-    ring(2, 3)
     ring(0, 4)
     ring(1, 4)
-    ring(3, 3)
     remote(pair_out, pair_in, tsend.at[1], trecv.at[1], at["far"]).wait_recv()
     lg[mine, :] = (pair_out[...].astype(f32) + pair_in[...].astype(f32)).astype(bf16)
     go(remote(lg.at[mine], lg.at[mine], tsend.at[2], trecv.at[2], at["core"]))
-    ring(2, 4)
-    ring(3, 4)
     sums_q, sums_v, sums_u, ends = sums
     triu = jnp.where(iota((256, 256), 0) <= iota((256, 256), 1), 1.0, 0.0).astype(bf16)
     lower = jnp.where(iota((256, 256), 0) > iota((256, 256), 1), 1.0, 0.0).astype(bf16)
@@ -619,8 +614,12 @@
         copy.wait_send()
     for e in (f1, f2, b1, b2):
         e[2]()
-    finish(2)
-    finish(3)
+    sums_out[2][1]()
+    sums_out[2][2]()
+    ig[:, 0:256] = jnp.sum(d_got[0].astype(f32), axis=0)
+    sums_out[3][1]()
+    sums_out[3][2]()
+    ig[:, 256:512] = jnp.sum(d_got[1].astype(f32), axis=0)
     remote(lg.at[other], lg.at[other], tsend.at[2], trecv.at[2], at["core"]).wait_recv()
     for copy in sent:
         copy.wait_send()
@@ -653,9 +652,9 @@
             vm((3, 4, 256, 512)), vm((2, 4, 256, 512)),
             vm((256, 2048), f32), vm((128, 2048)), vm((128, 2048)), vm((128, 2048)), vm((128, 2048)),
             vm((3, 16, 32, 512), f32), vm((3, 7, 2, 32, 512)), vm((3, 7, 2, 32, 512)),
-            vm((3, 32, 512)), vm((3, 32, 512)),
+            vm((3, 32, 512)), vm((3, 32, 512)), vm((2, 16, 32, 256)), vm((2, 16, 32, 256)),
             dma((3, 12)), dma((3, 12)), dma((2, 4)), dma((2, 4)), dma((2, 4, 3)), dma((2, 4, 3)),
-            dma((4, 16)), dma((4, 16)),
+            dma((6, 16)), dma((6, 16)),
             dma((4, 6)), dma((4, 6)), dma((4, 7)), dma((4, 7)), dma((4,)), dma((4,)), dma((3,)), dma((3,)),
             dma((4,)),
         ],

time: 113 us -> 111 us (0.982); the launches traced: 113 us -> 110 us
  Pallas kernels: 108 us -> 104 us
    pallas_call x1, Pallas kernels: 105 us -> 102 us  [whole(): pl.pallas_call(kernel, out_shape=(jax.ShapeDtypeStruct((256, 2048), bf16)...]
where the time goes in v5:
time: 111 us; the launch traced here: 110 us
  Pallas kernels  104 us (94%)
  local copies, waits for them, and re-layouts  3.5 us (3%)
  between operations  1.93 us (2%)
    pallas_call x1, Pallas kernels, whole(): pl.pallas_call(kernel, out_shape=(jax.ShapeDtypeStruct((256, 2048), bf16)...  102 us
    unnamed x2, local copies, waits for them, and re-layouts  3.5 us
    pallas_call x1, Pallas kernels, settle(): pl.pallas_call(settle_kernel, out_shape=tuple((jax.ShapeDtypeStruct(*kind...  2.7 us

profile of v5, /device:TPU:16, one launch (start us, length us, event | category | flops | bytes accessed | tf_op | source)
XLA Modules:
  0.0 109.8 jit_solution(6735227975674169334)
XLA Ops:
  1.9 1.9 %copy.17 = bf16[64,8,2,256]{3,1,2,0:T(8,128)(2,1)} copy(bf16[64,8,2,256]{3,2,1,0:T(2,128)(2,1)} %bitcast.21) | data formatting | bytes 1048576
  3.8 101.7 %whole.1 = (bf16[256,2048]{1,0:T(8,128)(2,1)}, bf16[256,1024]{1,0:T(8,128)(2,1)}, f32[256,16]{1,0:T(8,128)}, f32[32,1024]{1,0:T(8,128)}, f32[32,512]{1,0:T(8,128)}) custom-call(bf16[256,1024]{1,0:T(8,128)(2,1)} %bitcast.22, f32[16,256]{1,0:T(8,128)} %bitcast.24, f32[1,16]{1,0:T(1,128)} %bitcast.25, f32[1,16]{1,0:T(1,128)} %bitcast.26, f32[1,16]{1,0:T(1,128)} %bitcast.27, ...), custom_call_target="tpu_custom_call" | custom-call | tf_op jit(solution)/shard_map/whole/pallas_call | solution.py:633
  105.5 2.7 %settle.1 = (bf16[256,2048]{1,0:T(8,128)(2,1)}, bf16[256,1024]{1,0:T(8,128)(2,1)}, f32[256,16]{1,0:T(8,128)}, f32[32,1024]{1,0:T(8,128)}, f32[32,2,256]{2,1,0:T(2,128)}) custom-call(bf16[256,2048]{1,0:T(8,128)(2,1)} %get-tuple-element.15.lg, bf16[256,1024]{1,0:T(8,128)(2,1)} %get-tuple-element.16.hg, f32[256,16]{1,0:T(8,128)} %get-tuple-element.17.sg, ...), custom_call_target="tpu_custom_call" | custom-call | tf_op jit(solution)/shard_map/settle/pallas_call | solution.py:679
  108.2 1.6 %copy.16 = f32[1,256,16]{1,2,0:T(8,128)} copy(f32[1,256,16]{2,1,0:T(8,128)} %bitcast.23) | data formatting | bytes 32768

commit v6 on v5

--- a/solution.py
+++ b/solution.py
@@ -676,11 +676,17 @@
 
 def settle(*found):
     shapes = [(v.shape, v.dtype) for v in found[:4]] + [((32, 2, 256), f32)]
+
+    def rows(shape):
+        rest = tuple(shape[1:])
+        return pl.BlockSpec((shape[0] // 4,) + rest, lambda n: (n,) + (0,) * len(rest))
+
     return pl.pallas_call(
         settle_kernel,
         out_shape=tuple(jax.ShapeDtypeStruct(*kind) for kind in shapes),
-        in_specs=[VM] * 5,
-        out_specs=(VM,) * 5,
+        grid=(4,),
+        in_specs=[rows(v.shape) for v in found],
+        out_specs=tuple(rows(shape) for shape, _ in shapes),
         name="settle",
     )(*found)
 

time: 111 us -> 112 us (level)
  no operation moved by 1% of the time
where the time goes in v6:
time: 112 us; the launch traced here: 111 us
  Pallas kernels  105 us (94%)
  local copies, waits for them, and re-layouts  3.5 us (3%)
  between operations  1.94 us (2%)
    pallas_call x1, Pallas kernels, whole(): pl.pallas_call(kernel, out_shape=(jax.ShapeDtypeStruct((256, 2048), bf16)...  102 us
    pallas_call x1, Pallas kernels, settle(): pl.pallas_call(settle_kernel, out_shape=tuple((jax.ShapeDtypeStruct(*kind...  3.71 us
    unnamed x2, local copies, waits for them, and re-layouts  3.5 us

profile of v6, /device:TPU:16, one launch (start us, length us, event | category | flops | bytes accessed | tf_op | source)
XLA Modules:
  0.0 110.8 jit_solution(13361644248999250852)
XLA Ops:
  1.9 1.9 %copy.17 = bf16[64,8,2,256]{3,1,2,0:T(8,128)(2,1)} copy(bf16[64,8,2,256]{3,2,1,0:T(2,128)(2,1)} %bitcast.21) | data formatting | bytes 1048576
  3.8 101.7 %whole.1 = (bf16[256,2048]{1,0:T(8,128)(2,1)}, bf16[256,1024]{1,0:T(8,128)(2,1)}, f32[256,16]{1,0:T(8,128)}, f32[32,1024]{1,0:T(8,128)}, f32[32,512]{1,0:T(8,128)}) custom-call(bf16[256,1024]{1,0:T(8,128)(2,1)} %bitcast.22, f32[16,256]{1,0:T(8,128)} %bitcast.24, f32[1,16]{1,0:T(1,128)} %bitcast.25, f32[1,16]{1,0:T(1,128)} %bitcast.26, f32[1,16]{1,0:T(1,128)} %bitcast.27, ...), custom_call_target="tpu_custom_call" | custom-call | tf_op jit(solution)/shard_map/whole/pallas_call | solution.py:633
  105.5 3.7 %settle.1 = (bf16[256,2048]{1,0:T(8,128)(2,1)}, bf16[256,1024]{1,0:T(8,128)(2,1)}, f32[256,16]{1,0:T(8,128)}, f32[32,1024]{1,0:T(8,128)}, f32[32,2,256]{2,1,0:T(2,128)}) custom-call(bf16[256,2048]{1,0:T(8,128)(2,1)} %get-tuple-element.15.lg, bf16[256,1024]{1,0:T(8,128)(2,1)} %get-tuple-element.16.hg, f32[256,16]{1,0:T(8,128)} %get-tuple-element.17.sg, ...), custom_call_target="tpu_custom_call" | custom-call | tf_op jit(solution)/shard_map/settle/pallas_call | solution.py:684
  109.2 1.6 %copy.16 = f32[1,256,16]{1,2,0:T(8,128)} copy(f32[1,256,16]{2,1,0:T(8,128)} %bitcast.23) | data formatting | bytes 32768
